TPU v7x, 128 devices: a whole 4x4x4 slice. The times are simulated.
128 devices in a mesh: grp: 4 (over z_hi, core), row: 32 (over z_lo, y, x).
Axes of the slice: x: 4, y: 4, z: 4 (z_hi: 2, z_lo: 2; z = z_hi * 2 + z_lo), core: 2. Of those that a mesh axis runs over, the one named last changes fastest.
Arguments:
- pair: bfloat16 [1024, 1024, 128], P('row', 'grp'), may hold values from -6 to 6
- token_mask: int32 [1024], replicated, may hold values 0 or 1
- in_gain: float32 [128], replicated, may hold values from 0.5 to 1.5
- in_bias: float32 [128], replicated, may hold values from -3 to 3
- w_in: bfloat16 [128, 512], replicated, may hold values from -0.5 to 0.5
- w_gate: bfloat16 [128, 128], replicated, may hold values from -0.5 to 0.5
- out_gain: float32 [128], replicated, may hold values from 0.5 to 1.5
- out_bias: float32 [128], replicated, may hold values from -3 to 3
- w_out: bfloat16 [128, 128], replicated, may hold values from -0.5 to 0.5
- d_update: bfloat16 [1024, 1024, 128], P('row', 'grp'), may hold values from -6 to 6
Outputs:
- update: bfloat16 [1024, 1024, 128], P('row', 'grp')
- d_pair: bfloat16 [1024, 1024, 128], P('row', 'grp')
- d_w_in: float32 [128, 512], replicated
- d_w_gate: float32 [128, 128], replicated
- d_w_out: float32 [128, 128], replicated
- d_in_norm: float32 [2, 128], replicated
- d_out_norm: float32 [2, 128], replicated
Inputs may be any that keep to these rules, and one draw needn't show every extreme that they name: `token_mask`: 1 marks a real token, 0 a padding token.
All inputs are finite; a program needn't handle non-finite values.
Results may differ from a plain program's by a relative error of at most 0.0068.
Values may be sent and summed in bfloat16 or wider, within the bound.
No kernel may reach another device: no remote copies, remote signals or barrier semaphores. Data moves between devices by JAX's collectives and lax.ppermute only.
A program may use at most 128 MiB of HBM per device.

v0:
```python
import jax
import jax.numpy as jnp
from jax import lax
from jax.sharding import PartitionSpec as P

EPS = 1e-05


def norm_along(values, axis):
    average = jnp.mean(values, axis=axis, keepdims=True)
    centered = values - average
    inv_std = lax.rsqrt(jnp.mean(centered * centered, axis=axis, keepdims=True) + EPS)
    return (centered * inv_std, inv_std)


def norm_back(grad_hat, normed_hat, inv_std, axis):
    return inv_std * (
        grad_hat
        - jnp.mean(grad_hat, axis=axis, keepdims=True)
        - normed_hat * jnp.mean(grad_hat * normed_hat, axis=axis, keepdims=True)
    )


def to_channels(stacked):
    copies, hidden, tile_rows, tile_cols = stacked.shape
    grid_cols = lax.axis_size("grp")
    grid_rows = lax.axis_size("row")
    per_device = hidden // (grid_cols * grid_rows)
    shaped = stacked.reshape(copies, grid_cols, grid_rows, per_device, tile_rows, tile_cols)
    arrived = lax.all_to_all(
        lax.all_to_all(shaped, "grp", split_axis=1, concat_axis=5, tiled=True),
        "row",
        split_axis=2,
        concat_axis=4,
        tiled=True,
    )
    return arrived.reshape(copies, per_device, grid_rows * tile_rows, grid_cols * tile_cols)


def to_tiles(stacked):
    copies, per_device, rows_all, cols_all = stacked.shape
    grid_cols = lax.axis_size("grp")
    grid_rows = lax.axis_size("row")
    tile_rows = rows_all // grid_rows
    tile_cols = cols_all // grid_cols
    hidden = per_device * grid_cols * grid_rows
    shaped = stacked.reshape(copies, 1, 1, per_device, rows_all, cols_all)
    arrived = lax.all_to_all(
        lax.all_to_all(shaped, "grp", split_axis=5, concat_axis=1, tiled=True),
        "row",
        split_axis=4,
        concat_axis=2,
        tiled=True,
    )
    return arrived.reshape(copies, hidden, tile_rows, tile_cols)


def body(pair, token_mask, in_gain, in_bias, w_in, w_gate, out_gain, out_bias, w_out, d_update):
    tile_rows, tile_cols, pair_width = pair.shape
    hidden = w_out.shape[0]
    mask_all = token_mask.astype(jnp.float32)
    row_mask = lax.dynamic_slice_in_dim(mask_all, lax.axis_index("row") * tile_rows, tile_rows)
    col_mask = lax.dynamic_slice_in_dim(mask_all, lax.axis_index("grp") * tile_cols, tile_cols)
    mask_pair = row_mask[:, None] * col_mask[None, :]
    pair_hat, inv_std = norm_along(pair.astype(jnp.float32), -1)
    normed = (pair_hat * in_gain + in_bias).astype(jnp.bfloat16)
    projected = jnp.einsum("rjc,cf->frj", normed, w_in, preferred_element_type=jnp.float32)
    projected = projected.reshape(2, 2, hidden, tile_rows, tile_cols)
    edge_gates = jax.nn.sigmoid(projected[:, 0])
    edge_values = projected[:, 1]
    edge_pairs = (edge_gates * edge_values * mask_pair).astype(jnp.bfloat16)
    channel_edges = to_channels(edge_pairs)
    triangle = jnp.einsum(
        "cki,ckj->cij", channel_edges[0], channel_edges[1], preferred_element_type=jnp.float32
    ).astype(jnp.bfloat16)
    tri_tile = to_tiles(triangle[None])[0]
    tri_hat, tri_inv = norm_along(tri_tile.astype(jnp.float32), 0)
    tri_norm = (tri_hat * out_gain[:, None, None] + out_bias[:, None, None]).astype(jnp.bfloat16)
    out_proj = jnp.einsum("crj,cd->rjd", tri_norm, w_out, preferred_element_type=jnp.float32)
    out_gate = jax.nn.sigmoid(
        jnp.einsum("rjc,cd->rjd", normed, w_gate, preferred_element_type=jnp.float32)
    )
    update = (out_gate * out_proj).astype(jnp.bfloat16)
    cotangent = d_update.astype(jnp.float32)
    d_proj = (cotangent * out_gate).astype(jnp.bfloat16)
    d_gate_pre = (cotangent * out_proj * out_gate * (1.0 - out_gate)).astype(jnp.bfloat16)
    sum_out = jnp.einsum("crj,rjd->cd", tri_norm, d_proj, preferred_element_type=jnp.float32)
    sum_gate = jnp.einsum("rjc,rjd->cd", normed, d_gate_pre, preferred_element_type=jnp.float32)
    d_tri_norm = jnp.einsum("rjd,cd->crj", d_proj, w_out, preferred_element_type=jnp.float32)
    sum_out_norm = jnp.stack(
        [jnp.sum(d_tri_norm * tri_hat, axis=(1, 2)), jnp.sum(d_tri_norm, axis=(1, 2))]
    )
    d_triangle = norm_back(d_tri_norm * out_gain[:, None, None], tri_hat, tri_inv, 0).astype(
        jnp.bfloat16
    )
    left_edges = channel_edges[0]
    right_edges = channel_edges[1]
    d_channel = to_channels(d_triangle[None])[0]
    d_left = jnp.einsum("ckj,cij->cki", right_edges, d_channel, preferred_element_type=jnp.float32)
    d_right = jnp.einsum("cki,cij->ckj", left_edges, d_channel, preferred_element_type=jnp.float32)
    d_edge_tiles = to_tiles(jnp.stack([d_left.astype(jnp.bfloat16), d_right.astype(jnp.bfloat16)]))
    d_edge_f = d_edge_tiles.astype(jnp.float32) * mask_pair
    d_gate_in = d_edge_f * edge_values * edge_gates * (1.0 - edge_gates)
    d_value_in = d_edge_f * edge_gates
    d_projected = (
        jnp.stack([d_gate_in, d_value_in], axis=1)
        .reshape(4 * hidden, tile_rows, tile_cols)
        .astype(jnp.bfloat16)
    )
    sum_in = jnp.einsum("rjc,frj->cf", normed, d_projected, preferred_element_type=jnp.float32)
    d_normed = jnp.einsum("frj,cf->rjc", d_projected, w_in, preferred_element_type=jnp.float32)
    d_normed = d_normed + jnp.einsum(
        "rjd,cd->rjc", d_gate_pre, w_gate, preferred_element_type=jnp.float32
    )
    sum_in_norm = jnp.stack(
        [jnp.sum(d_normed * pair_hat, axis=(0, 1)), jnp.sum(d_normed, axis=(0, 1))]
    )
    d_pair = norm_back(d_normed * in_gain, pair_hat, inv_std, -1).astype(jnp.bfloat16)
    totals = lax.psum((sum_in, sum_gate, sum_out, sum_in_norm, sum_out_norm), ("grp", "row"))
    scale = 1.0 / token_mask.shape[0]
    return (
        update,
        d_pair,
        totals[0] * scale,
        totals[1] * scale,
        totals[2] * scale,
        totals[3] * scale,
        totals[4] * scale,
    )


def solution(mesh):
    return jax.shard_map(
        body,
        mesh=mesh,
        in_specs=(
            P("row", "grp", None),
            P(),
            P(),
            P(),
            P(),
            P(),
            P(),
            P(),
            P(),
            P("row", "grp", None),
        ),
        out_specs=(P("row", "grp", None), P("row", "grp", None), P(), P(), P(), P(), P()),
        check_vma=False,
    )
```

profile of v0, /device:TPU:1, one launch (start us, length us, event | category | flops | bytes accessed | tf_op | source)
XLA Modules:
  0.0 860.0 jit_solution(5685136882153236722)
XLA Ops:
  10.4 3.6 fusion.19
  14.1 6.7 convolution_bitcast_fusion
  20.8 19.9 %reshape.220 = f32[2,2,128,32,256]{2,1,0,4,3:T(2,128)} reshape(f32[512,32,256]{0,2,1:T(8,128)} %convolution_bitcast_fusion) | data formatting | bytes 33554432 | tf_op jit(solution)/shard_map/reshape | solution.py:68
  40.7 19.3 %fusion.53 = (f32[2,1,128,32,256]{2,1,0,4,3:T(1,128)}, f32[2,1,128,32,256]{2,1,0,4,3:T(1,128)}) fusion(f32[2,2,128,32,256]{2,1,0,4,3:T(2,128)} %reshape.220), kind=kLoop, calls=%fused_computation.87 | loop fusion | bytes 33554432 | tf_op jit(solution)/shard_map/slice | solution.py:69
  60.0 13.3 %copy.105 = f32[2,1,128,32,256]{4,3,2,0,1:T(8,128)} copy(f32[2,1,128,32,256]{2,1,0,4,3:T(1,128)} %get-tuple-element.19) | data formatting | bytes 16777216
  73.3 13.3 %copy.106 = f32[2,1,128,32,256]{4,3,2,0,1:T(8,128)} copy(f32[2,1,128,32,256]{2,1,0,4,3:T(1,128)} %get-tuple-element.20) | data formatting | bytes 16777216
  86.7 7.0 fusion.52
  95.5 55.2 %all_to_all.108 = bf16[2,4,32,1,32,256]{5,4,2,0,3,1:T(8,128)(2,1)S(1)} all-to-all(bf16[2,4,32,1,32,256]{5,4,2,0,3,1:T(8,128)(2,1)S(1)} %copy.78), channel_id=1, replica_groups=mesh['grp'=4,'row'=32] {'grp'}, dimensions={1} | all-to-all | bytes 8388608 | tf_op jit(solution)/shard_map/all_to_all | solution.py:31
  150.8 10.2 %copy.102 = bf16[2,1,32,1,32,4,256]{6,5,4,0,2,3,1:T(4,128)(2,1)} copy(bf16[2,1,32,1,32,4,256]{6,4,2,0,5,3,1:T(8,128)(2,1)S(1)} %bitcast.126) | data formatting | bytes 8388608 | tf_op jit(solution)/shard_map/all_to_all | solution.py:31
  161.0 7.7 reshape.237
  168.7 56.5 %all_to_all.109 = bf16[2,1,32,1,32,1024]{5,4,3,1,0,2:T(8,128)(2,1)S(1)} all-to-all(bf16[2,1,32,1,32,1024]{5,4,3,1,0,2:T(8,128)(2,1)} %reshape.237), channel_id=1, replica_groups=mesh['grp'=4,'row'=32] {'row'}, dimensions={2} | all-to-all | bytes 8388608 | tf_op jit(solution)/shard_map/all_to_all | solution.py:30
  227.1 3.8 fusion.29
  230.9 10.9 %copy.83 = bf16[1,1,1,1,1024,1024]{4,3,2,1,0,5:T(2,128)(2,1)} copy(bf16[1,1,1,1,1024,1024]{5,4,3,2,1,0:T(8,128)(2,1)} %fusion.29) | data formatting | bytes 4194304 | tf_op jit(solution)/shard_map/reshape;broadcast_in_dim | solution.py:47
  242.3 14.1 %reduce.7 = bf16[1024,1024]{1,0:T(8,128)(2,1)} reduce(bf16[1024,1,1,1,1,1024]{5,4,3,2,1,0:T(2,128)(2,1)} %bitcast.123, bf16[]{:T(256)} %broadcast.167), dimensions={1,2,3,4}, to_apply=%bitcast.102.reduce_sub_computation | reduce | bytes 4194306
  256.4 4.5 reshape.238
  260.9 33.4 %all_to_all.110 = bf16[4,2,131072]{2,1,0:T(2,128)(2,1)} all-to-all(bf16[4,2,131072]{2,1,0:T(2,128)(2,1)} %reshape.238), channel_id=1, replica_groups=mesh['grp'=4,'row'=32] {'grp'}, dimensions={0} | all-to-all | bytes 4194304 | tf_op jit(solution)/shard_map/all_to_all | solution.py:49
  294.2 5.0 reshape.239
  299.2 4.3 copy.104
  303.5 4.2 copy.84
  307.8 5.2 all-to-all-start.3
  313.0 4.3 add_divide_fusion.1
  317.2 22.5 %all-to-all-done.3 = bf16[1,4,1,1,1024,256]{5,1,3,2,0,4:T(4,128)(2,1)} async-done(((bf16[1,4,1,1,1024,256]{5,1,3,2,0,4:T(4,128)(2,1)}), bf16[1,4,1,1,1024,256]{5,1,3,2,0,4:T(4,128)(2,1)}, u32[]{:S(2)}, u32[]{:S(2)}) %all-to-all-start.3) | async-done | bytes 2097184 | tf_op jit(solution)/shard_map/all_to_all | solution.py:48
  347.7 3.3 fusion.24
  351.1 6.5 multiply_convert_fusion.1
  358.8 30.8 %all_to_all.111 = bf16[1,4,32,1,32,256]{5,4,2,3,0,1:T(8,128)(2,1)S(1)} all-to-all(bf16[1,4,32,1,32,256]{5,4,2,3,0,1:T(8,128)(2,1)S(1)} %copy.88), channel_id=1, replica_groups=mesh['grp'=4,'row'=32] {'grp'}, dimensions={1} | all-to-all | bytes 4194304 | tf_op jit(solution)/shard_map/all_to_all | solution.py:31
  391.3 4.9 all-to-all-start.5
  396.2 5.0 fusion.54
  401.3 21.7 %all-to-all-done.5 = bf16[1,1,32,1,32,1024]{5,4,3,1,0,2:T(8,128)(2,1)} async-done(((bf16[1,1,32,1,32,1024]{5,4,3,1,0,2:T(8,128)(2,1)}), bf16[1,1,32,1,32,1024]{5,4,3,1,0,2:T(8,128)(2,1)}, u32[]{:S(2)}, u32[]{:S(2)}) %all-to-all-start.5) | async-done | bytes 2097184 | tf_op jit(solution)/shard_map/all_to_all | solution.py:30
  422.9 4.7 convert_bitcast_fusion
  427.6 4.0 convert_bitcast_fusion.1
  434.0 11.3 %copy.91 = bf16[2,1,1,1,1024,1024]{4,0,3,2,1,5:T(2,128)(2,1)} copy(bf16[2,1,1,1,1024,1024]{5,4,0,3,2,1:T(8,128)(2,1)} %maximum_bitcast_fusion) | data formatting | bytes 8388608 | tf_op jit(solution)/shard_map/reshape | solution.py:47
  445.3 56.6 %all_to_all.112 = bf16[2,1,1,1,1024,1024]{4,0,3,2,1,5:T(2,128)(2,1)} all-to-all(bf16[2,1,1,1,1024,1024]{4,0,3,2,1,5:T(2,128)(2,1)} %copy.91), channel_id=1, replica_groups=mesh['grp'=4,'row'=32] {'grp'}, dimensions={5} | all-to-all | bytes 8388608 | tf_op jit(solution)/shard_map/all_to_all | solution.py:49
  501.9 11.8 %copy.92 = bf16[2,1,1,1,1024,4,256]{6,5,0,4,3,2,1:T(4,128)(2,1)} copy(bf16[2,1,1,1,1024,4,256]{4,0,6,5,3,2,1:T(2,128)(2,1)} %bitcast.127) | data formatting | bytes 8388608 | tf_op jit(solution)/shard_map/all_to_all | solution.py:49
  513.7 4.9 all-to-all-start.7
  521.2 6.2 fusion.23
  528.7 3.6 convolution_bitcast_fusion.3
  533.8 34.7 %all-to-all-done.7 = bf16[2,4,1,1,1024,256]{5,1,0,3,2,4:T(4,128)(2,1)} async-done(((bf16[2,4,1,1,1024,256]{5,1,0,3,2,4:T(4,128)(2,1)}), bf16[2,4,1,1,1024,256]{5,1,0,3,2,4:T(4,128)(2,1)}, u32[]{:S(2)}, u32[]{:S(2)}) %all-to-all-start.7) | async-done | bytes 4194336 | tf_op jit(solution)/shard_map/all_to_all | solution.py:48
  568.6 3.0 copy.93
  571.6 10.2 %fusion.4 = (bf16[2,1,128,32,256]{4,3,2,0,1:T(8,128)(2,1)}, bf16[2,1,128,32,256]{4,3,2,0,1:T(8,128)(2,1)}) fusion(f32[2,1,128,32,256]{4,3,2,0,1:T(8,128)} %copy.106, bf16[2,1,128,32,256]{4,3,2,0,1:T(8,128)(2,1)S(1)} %bitcast.128, f32[32,256]{1,0:T(8,128)S(1)} %broadcast_multiply_fusion.3, f32[2,1,128,32,256]{4,3,2,0,1:T(8,128)} %copy.105), kind=kLoop, calls=%fused_computation.7 | loop fusion | flops 25165824 | bytes 29392896 | tf_op jit(solution)/shard_map/convert.2
  581.8 7.5 pad_maximum_fusion
  589.2 15.6 %copy.94 = bf16[2,2,128,32,256]{2,1,0,4,3:T(2,128)(2,1)} copy(bf16[2,2,128,32,256]{4,3,2,0,1:T(8,128)(2,1)} %pad_maximum_fusion) | data formatting | bytes 16777216 | tf_op jit(solution)/shard_map/stack | solution.py:106
  604.8 13.1 %convert_element_type.102 = bf16[512,32,256]{0,2,1:T(8,128)(2,1)} reshape(bf16[2,2,128,32,256]{2,1,0,4,3:T(2,128)(2,1)} %copy.94) | data formatting | bytes 16777216 | tf_op jit(solution)/shard_map/convert_element_type | solution.py:108
  617.9 7.4 convolution_bitcast_fusion.1
  625.3 5.9 fusion.35
  631.2 6.6 fusion.18
  637.8 67.6 %all-reduce = (f32[2,128]{1,0:T(2,128)S(1)}, f32[2,128]{1,0:T(2,128)S(1)}) all-reduce(f32[2,128]{1,0:T(2,128)S(1)} %pad_maximum_fusion.1, f32[2,128]{1,0:T(2,128)S(1)} %pad_maximum_fusion.2), channel_id=1, replica_groups=mesh['grp'=4,'row'=32] {'grp','row'}, use_global_device_ids=true, to_apply=%region_15.0 | all-reduce | flops 512 | bytes 4096 | tf_op jit(solution)/shard_map/psum | solution.py:119
  706.0 8.4 fusion.17
  715.0 133.2 %all-reduce.4.cloned.1.call-done = (f32[128,512]{1,0:T(8,128)}, f32[128,128]{1,0:T(8,128)}, f32[128,128]{1,0:T(8,128)}) async-done(((f32[128,512]{1,0:T(8,128)}, f32[128,128]{1,0:T(8,128)}, f32[128,128]{1,0:T(8,128)}), (f32[128,512]{1,0:T(8,128)}, f32[128,128]{1,0:T(8,128)}, f32[128,128]{1,0:T(8,128)})) %all-reduce.4.cloned.1.call-update) | async-done | bytes 393232 | tf_op jit(solution)/shard_map/psum | solution.py:119
  (71 shorter events, 31.8 us)
Async XLA Ops:
  7.2 6.9 copy-start
  7.2 6.9 copy-start.1
  7.2 6.9 copy-start.14
  7.2 6.9 copy-start.16
  225.2 2.0 copy-start.8
  303.5 9.4 %copy-start.13 = (bf16[128,128]{1,0:T(8,128)(2,1)S(1)}, bf16[128,128]{1,0:T(8,128)(2,1)}, u32[]{:S(2)}) copy-start(bf16[128,128]{1,0:T(8,128)(2,1)} %param.15) | copy-start | bytes 98308
  307.8 32.0 %all-to-all-start.3 = ((bf16[1,4,1,1,1024,256]{5,1,3,2,0,4:T(4,128)(2,1)}), bf16[1,4,1,1,1024,256]{5,1,3,2,0,4:T(4,128)(2,1)}, u32[]{:S(2)}, u32[]{:S(2)}) async-start(bf16[1,4,1,1,1024,256]{5,1,3,2,0,4:T(4,128)(2,1)} %copy.84), calls=%async_computation.3 | async-start | bytes 4194304 | tf_op jit(solution)/shard_map/all_to_all | solution.py:48
  344.1 2.2 copy-start.12
  344.1 2.2 copy-start.15
  344.2 2.8 copy-start.2
  344.2 3.5 copy-start.6
  347.7 3.4 copy-start.17
  351.1 6.6 copy-start.4
  391.3 31.7 %all-to-all-start.5 = ((bf16[1,1,32,1,32,1024]{5,4,3,1,0,2:T(8,128)(2,1)}), bf16[1,1,32,1,32,1024]{5,4,3,1,0,2:T(8,128)(2,1)}, u32[]{:S(2)}, u32[]{:S(2)}) async-start(bf16[1,1,32,1,32,1024]{5,4,3,1,0,2:T(8,128)(2,1)} %bitcast.131), calls=%async_computation.5 | async-start | bytes 4194304 | tf_op jit(solution)/shard_map/all_to_all | solution.py:30
  422.9 4.7 copy-start.11
  513.7 54.8 %all-to-all-start.7 = ((bf16[2,4,1,1,1024,256]{5,1,0,3,2,4:T(4,128)(2,1)}), bf16[2,4,1,1,1024,256]{5,1,0,3,2,4:T(4,128)(2,1)}, u32[]{:S(2)}, u32[]{:S(2)}) async-start(bf16[2,4,1,1,1024,256]{5,1,0,3,2,4:T(4,128)(2,1)} %bitcast.125), calls=%async_computation.7 | async-start | bytes 8388608 | tf_op jit(solution)/shard_map/all_to_all | solution.py:48
  518.6 329.7 %all-reduce.4.cloned.1.call-start = ((), (), s32[]{:S(2)}) async-start(), calls=%async_computation.8 | async-start | bytes 786432 | tf_op jit(solution)/shard_map/psum | solution.py:119
  521.1 11.2 %copy-start.7 = (bf16[32,256,128]{2,1,0:T(8,128)(2,1)S(1)}, bf16[32,256,128]{2,1,0:T(8,128)(2,1)}, u32[]{:S(2)}) copy-start(bf16[32,256,128]{2,1,0:T(8,128)(2,1)} %param.19) | copy-start | bytes 6291460
  527.4 1.3 copy-start.9
  527.4 5.0 copy-start.3
  527.4 5.0 copy-start.5
  625.3 5.9 copy-start.10
Sparse Core Ops, SparseCore 0:
  706.2 142.0 all-reduce.3
where the time goes:
time: 870 us; the launch traced here: 860 us
  blocking collectives  300 us (34%)
  waiting for transfers between devices  212 us (24%)
  local copies, waits for them, and re-layouts  181 us (21%)
  other arithmetic  78.7 us (9%)
  matrix products  58 us (7%)
  starting transfers between devices  15 us (2%)
  between operations  14.6 us (2%)
    psum x1, waiting for transfers between devices, body(): lax.psum((sum_in, sum_gate, sum_out, sum_in_norm, sum_out_norm), ('grp',...  133 us
    all_to_all x2, blocking collectives, to_tiles(): lax.all_to_all(shaped, 'grp', split_axis=5, concat_axis=1, tiled=True)  90 us
    all_to_all x2, blocking collectives, to_channels(): lax.all_to_all(shaped, 'grp', split_axis=1, concat_axis=5, tiled=True)  86.1 us
    psum x1, blocking collectives, body(): lax.psum((sum_in, sum_gate, sum_out, sum_in_norm, sum_out_norm), ('grp',...  67.6 us
    all_to_all x2, waiting for transfers between devices, to_tiles(): lax.all_to_all(lax.all_to_all(shaped, 'grp', split_axis=5, concat_axis=1,...  57.2 us
    all_to_all x1, blocking collectives, to_channels(): lax.all_to_all(lax.all_to_all(shaped, 'grp', split_axis=1, concat_axis=5,...  56.5 us
    unnamed x42, local copies, waits for them, and re-layouts  45.6 us
    all_to_all x1, waiting for transfers between devices, to_channels(): lax.all_to_all(lax.all_to_all(shaped, 'grp', split_axis=1, concat_axis=5,...  21.7 us
  transfers between devices with their start and end apart: 4, of which 4 were waited for; matrix products, arithmetic and copies ran while one was open for 4% of the time, Pallas kernels for 0%

commit v1 on v0

v1 whole, which is shorter than its diff:
```python
import functools

import jax
import jax.numpy as jnp
from jax import lax
from jax.experimental import pallas as pl
from jax.experimental.pallas import tpu as pltpu
from jax.sharding import PartitionSpec as P

EPS = 1e-05
AXES = ("grp", "row")
RB = 16
F32 = jnp.float32
BF16 = jnp.bfloat16


def dot(lhs, rhs):
    return jnp.dot(lhs, rhs, preferred_element_type=F32)


def dot_nt(lhs, rhs):
    return lax.dot_general(lhs, rhs, (((1,), (1,)), ((), ())), preferred_element_type=F32)


def sigmoid(x):
    return 0.5 + 0.5 * jnp.tanh(0.5 * x)


def columns(vec_row, width):
    chans = vec_row.shape[1]
    return jnp.broadcast_to(vec_row, (width, chans)).T


def norm0(values):
    average = jnp.mean(values, axis=0, keepdims=True)
    centered = values - average
    inv_std = lax.rsqrt(jnp.mean(centered * centered, axis=0, keepdims=True) + EPS)
    return centered * inv_std, inv_std


def norm0_back(grad_hat, normed_hat, inv_std):
    return inv_std * (
        grad_hat
        - jnp.mean(grad_hat, axis=0, keepdims=True)
        - normed_hat * jnp.mean(grad_hat * normed_hat, axis=0, keepdims=True)
    )


def put_rows(scratch, slot, r, values):
    chans, width = values.shape
    for h in range(width // 128):
        scratch[slot + h, pl.ds(r, chans, stride=RB), :] = values[:, h * 128 : (h + 1) * 128]


def get_rows(scratch, slot, r, chans, width):
    return jnp.concatenate(
        [scratch[slot + h, pl.ds(r, chans, stride=RB), :] for h in range(width // 128)], axis=1
    )


def call(kernel, name, grid, ins, outs, scratch, flops, nbytes, args):
    return pl.pallas_call(
        kernel,
        name=name,
        grid=grid,
        in_specs=ins,
        out_specs=[spec for spec, _ in outs],
        out_shape=[shape for _, shape in outs],
        scratch_shapes=scratch,
        compiler_params=pltpu.CompilerParams(vmem_limit_bytes=60 * 1024 * 1024),
        cost_estimate=pl.CostEstimate(flops=flops, bytes_accessed=nbytes, transcendentals=0),
    )(*args)


def whole(shape):
    return pl.BlockSpec(shape, lambda *_: (0,) * len(shape))


def edges_kernel(pair, mask, gain, bias, w_in, edges, pair_t, scr, w_t, cols):
    chans = pair.shape[2]
    width = pair.shape[1]
    hidden = edges.shape[0]

    @pl.when(pl.program_id(0) == 0)
    def _():
        w_t[...] = w_in[...].T
        cols[0] = columns(gain[...], width)
        cols[1] = columns(bias[...], width)

    def step(r, carry):
        x_t = pair[r].T
        pair_t[r] = x_t
        hat, _ = norm0(x_t.astype(F32))
        normed = (hat * cols[0] + cols[1]).astype(BF16)
        proj = dot(w_t[...], normed)
        m = mask[pl.ds(r, 1), :]
        for side in range(2):
            gate = sigmoid(proj[side * 2 * hidden : (side * 2 + 1) * hidden])
            value = proj[(side * 2 + 1) * hidden : (side * 2 + 2) * hidden]
            put_rows(scr, side * (width // 128), r, gate * value * m)
        return carry

    lax.fori_loop(0, RB, step, 0, unroll=2)
    for side in range(2):
        for h in range(width // 128):
            edges[:, side, :, h * 128 : (h + 1) * 128] = (
                scr[side * (width // 128) + h].reshape(hidden, RB, 128).astype(BF16)
            )


def cotangent_kernel(pair_t, d_update, gain, bias, w_gate, d_proj, wg_t, cols):
    width = pair_t.shape[2]

    @pl.when(pl.program_id(0) == 0)
    def _():
        wg_t[...] = w_gate[...].T
        cols[0] = columns(gain[...], width)
        cols[1] = columns(bias[...], width)

    def step(r, carry):
        hat, _ = norm0(pair_t[r].astype(F32))
        normed = (hat * cols[0] + cols[1]).astype(BF16)
        gate = sigmoid(dot(wg_t[...], normed))
        d_proj[r] = (d_update[r].T.astype(F32) * gate).astype(BF16)
        return carry

    lax.fori_loop(0, RB, step, 0, unroll=2)


def triangle_kernel(left, right, out):
    groups, rows, _, tile_rows, width = right.shape
    depth = rows * tile_rows
    left_t = left[...].reshape(depth, width).T
    for h in range(groups):
        out[h] = dot(left_t, right[h].reshape(depth, width)).astype(BF16)


def d_tri_kernel(tri, d_proj, gain, w_out, d_tri, tri_t, scr_in, scr_out, cols):
    hidden, _, width = tri.shape
    halves = width // 128

    @pl.when(pl.program_id(0) == 0)
    def _():
        cols[...] = columns(gain[...], width)

    for h in range(halves):
        scr_in[h] = tri[:, :, h * 128 : (h + 1) * 128].astype(F32).reshape(hidden * RB, 128)

    def step(r, carry):
        t = get_rows(scr_in, 0, r, hidden, width)
        tri_t[r] = t.astype(BF16)
        hat, inv = norm0(t)
        grad = dot(w_out[...], d_proj[r]) * cols[...]
        put_rows(scr_out, 0, r, norm0_back(grad, hat, inv))
        return carry

    lax.fori_loop(0, RB, step, 0, unroll=2)
    for h in range(halves):
        d_tri[:, :, h * 128 : (h + 1) * 128] = (
            scr_out[h].reshape(hidden, RB, 128).astype(BF16)
        )


def update_kernel(
    tri_t, pair_t, d_update, gain, bias, w_gate, o_gain, o_bias, w_out,
    update, d_gate, sum_gate, sum_out, sum_norm,
    wg_t, wo_t, cols, acc,
):
    hidden, width = tri_t.shape[1:]

    @pl.when(pl.program_id(0) == 0)
    def _():
        wg_t[...] = w_gate[...].T
        wo_t[...] = w_out[...].T
        cols[0] = columns(gain[...], width)
        cols[1] = columns(bias[...], width)
        cols[2] = columns(o_gain[...], width)
        cols[3] = columns(o_bias[...], width)
        acc[...] = jnp.zeros_like(acc)
        sum_gate[...] = jnp.zeros_like(sum_gate)
        sum_out[...] = jnp.zeros_like(sum_out)

    def step(r, carry):
        hat, _ = norm0(pair_t[r].astype(F32))
        normed = (hat * cols[0] + cols[1]).astype(BF16)
        gate = sigmoid(dot(wg_t[...], normed))
        cot = d_update[r].T.astype(F32)
        d_proj = (cot * gate).astype(BF16)
        tri_hat, _ = norm0(tri_t[r].astype(F32))
        tri_norm = (tri_hat * cols[2] + cols[3]).astype(BF16)
        out_proj = dot(wo_t[...], tri_norm)
        update[r] = (gate * out_proj).astype(BF16).T
        d_gate_pre = (cot * out_proj * gate * (1.0 - gate)).astype(BF16)
        d_gate[r] = d_gate_pre
        sum_out[...] += dot_nt(tri_norm, d_proj)
        sum_gate[...] += dot_nt(normed, d_gate_pre)
        d_tri_norm = dot(w_out[...], d_proj)
        acc[0] += d_tri_norm * tri_hat
        acc[1] += d_tri_norm
        return carry

    lax.fori_loop(0, RB, step, 0, unroll=2)

    @pl.when(pl.program_id(0) == pl.num_programs(0) - 1)
    def _():
        lane = lax.broadcasted_iota(jnp.int32, (hidden, 128), 1)
        first = jnp.sum(acc[0], axis=1, keepdims=True)
        second = jnp.sum(acc[1], axis=1, keepdims=True)
        sum_norm[...] = jnp.where(lane == 2, first, jnp.where(lane == 3, second, 0.0))


def d_edges_kernel(edges, d_tri, out):
    groups, rows, _, tile_rows, width = edges.shape
    depth = rows * tile_rows
    for g in range(groups):
        left = jnp.zeros((depth, width), F32)
        right = jnp.zeros((depth, width), F32)
        for h in range(groups):
            left += dot_nt(
                edges[h, :, 1].reshape(depth, width), d_tri[h, g * width : (g + 1) * width, :]
            )
            right += dot(
                edges[h, :, 0].reshape(depth, width), d_tri[g, h * width : (h + 1) * width, :]
            )
        out[g, :, 0] = left.astype(BF16).reshape(rows, tile_rows, width)
        out[g, :, 1] = right.astype(BF16).reshape(rows, tile_rows, width)


def back_kernel(
    d_edges, pair_t, d_gate, mask, gain, bias, w_in, w_gate, sum_gate, sum_out, sum_norm,
    d_pair, sums,
    scr, w_t, w_all, cols, acc, acc_in,
):
    hidden = d_edges.shape[0]
    chans, width = pair_t.shape[1:]
    halves = width // 128

    @pl.when(pl.program_id(0) == 0)
    def _():
        w_t[...] = w_in[...].T
        w_all[:, : 4 * hidden] = w_in[...]
        w_all[:, 4 * hidden :] = w_gate[...]
        cols[0] = columns(gain[...], width)
        cols[1] = columns(bias[...], width)
        acc[...] = jnp.zeros_like(acc)
        acc_in[...] = jnp.zeros_like(acc_in)

    for side in range(2):
        for h in range(halves):
            scr[side * halves + h] = (
                d_edges[:, side, :, h * 128 : (h + 1) * 128].astype(F32).reshape(hidden * RB, 128)
            )

    def step(r, carry):
        hat, inv = norm0(pair_t[r].astype(F32))
        normed = (hat * cols[0] + cols[1]).astype(BF16)
        proj = dot(w_t[...], normed)
        m = mask[pl.ds(r, 1), :]
        parts = []
        for side in range(2):
            gate = sigmoid(proj[side * 2 * hidden : (side * 2 + 1) * hidden])
            value = proj[(side * 2 + 1) * hidden : (side * 2 + 2) * hidden]
            d_value = get_rows(scr, side * halves, r, hidden, width) * m * gate
            parts.append((d_value * value * (1.0 - gate)).astype(BF16))
            parts.append(d_value.astype(BF16))
        d_projected = jnp.concatenate(parts, axis=0)
        acc_in[...] += dot_nt(normed, d_projected)
        d_normed = dot(w_all[...], jnp.concatenate([d_projected, d_gate[r]], axis=0))
        acc[0] += d_normed * hat
        acc[1] += d_normed
        d_pair[r] = norm0_back(d_normed * cols[0], hat, inv).astype(BF16).T
        return carry

    lax.fori_loop(0, RB, step, 0, unroll=2)

    @pl.when(pl.program_id(0) == pl.num_programs(0) - 1)
    def _():
        lane = lax.broadcasted_iota(jnp.int32, (hidden, 128), 1)
        first = jnp.sum(acc[0], axis=1, keepdims=True)
        second = jnp.sum(acc[1], axis=1, keepdims=True)
        norms = jnp.where(lane == 0, first, jnp.where(lane == 1, second, sum_norm[...]))
        for q in range(4):
            sums[pl.ds(q, chans, stride=8), :] = acc_in[:, q * 128 : (q + 1) * 128]
        sums[pl.ds(4, chans, stride=8), :] = sum_gate[...]
        sums[pl.ds(5, chans, stride=8), :] = sum_out[...]
        sums[pl.ds(6, chans, stride=8), :] = norms
        sums[pl.ds(7, chans, stride=8), :] = norms


def total_kernel(scale, arrived, out):
    out[...] = jnp.broadcast_to(
        jnp.sum(arrived[...], axis=0, keepdims=True) * scale, out.shape
    )


def unpack_kernel(sums, d_w_in, d_w_gate, d_w_out, d_in_norm, d_out_norm):
    chans = d_w_in.shape[0]
    for q in range(4):
        d_w_in[:, q * 128 : (q + 1) * 128] = sums[pl.ds(q, chans, stride=8), :]
    d_w_gate[...] = sums[pl.ds(4, chans, stride=8), :]
    d_w_out[...] = sums[pl.ds(5, chans, stride=8), :]
    norms = sums[pl.ds(6, chans, stride=8), :].T
    d_in_norm[...] = norms[0:2]
    d_out_norm[...] = norms[2:4]


def exchange(chunks):
    return lax.all_to_all(chunks, AXES, split_axis=0, concat_axis=0, tiled=True)


def body(pair, token_mask, in_gain, in_bias, w_in, w_gate, out_gain, out_bias, w_out, d_update):
    tile_rows, tile_cols, chans = pair.shape
    hidden = w_out.shape[0]
    groups = lax.axis_size("grp")
    rows = lax.axis_size("row")
    tokens = token_mask.shape[0]
    devices = groups * rows
    steps = tile_rows // RB
    halves = tile_cols // 128
    positions = tile_rows * tile_cols
    sds = jax.ShapeDtypeStruct

    mask_all = token_mask.astype(F32)
    row_mask = lax.dynamic_slice_in_dim(mask_all, lax.axis_index("row") * tile_rows, tile_rows)
    col_mask = lax.dynamic_slice_in_dim(mask_all, lax.axis_index("grp") * tile_cols, tile_cols)
    mask_pair = row_mask[:, None] * col_mask[None, :]
    gain, bias = in_gain[None], in_bias[None]
    o_gain, o_bias = out_gain[None], out_bias[None]

    vec = whole((1, chans))
    square = whole((chans, hidden))
    wide = whole((chans, 4 * hidden))
    rowblock = pl.BlockSpec((RB, tile_cols, chans), lambda s: (s, 0, 0))
    chanblock = pl.BlockSpec((RB, chans, tile_cols), lambda s: (s, 0, 0))
    maskblock = pl.BlockSpec((RB, tile_cols), lambda s: (s, 0))
    edgeblock = pl.BlockSpec((hidden, 2, RB, tile_cols), lambda s: (0, 0, s, 0))
    triblock = pl.BlockSpec((hidden, RB, tile_cols), lambda s: (0, s, 0))
    t_shape = sds((tile_rows, chans, tile_cols), BF16)

    edges, pair_t = call(
        edges_kernel, "edges", (steps,),
        [rowblock, maskblock, vec, vec, wide],
        [(edgeblock, sds((hidden, 2, tile_rows, tile_cols), BF16)), (chanblock, t_shape)],
        [
            pltpu.VMEM((2 * halves, hidden * RB, 128), F32),
            pltpu.VMEM((4 * hidden, chans), BF16),
            pltpu.VMEM((2, chans, tile_cols), F32),
        ],
        2 * positions * chans * 4 * hidden, 16 * positions * chans,
        (pair, mask_pair, gain, bias, w_in),
    )
    chan_edges = exchange(edges)
    (d_proj,) = call(
        cotangent_kernel, "cotangent", (steps,),
        [chanblock, rowblock, vec, vec, square],
        [(chanblock, t_shape)],
        [pltpu.VMEM((chans, hidden), BF16), pltpu.VMEM((2, chans, tile_cols), F32)],
        2 * positions * chans * hidden, 8 * positions * chans,
        (pair_t, d_update, gain, bias, w_gate),
    )
    chan_edges = chan_edges.reshape(groups, rows, 2, tile_rows, tile_cols)
    (triangle,) = call(
        triangle_kernel, "triangle", (groups,),
        [
            pl.BlockSpec((1, rows, 1, tile_rows, tile_cols), lambda g: (g, 0, 0, 0, 0)),
            pl.BlockSpec((groups, rows, 1, tile_rows, tile_cols), lambda g: (0, 0, 1, 0, 0)),
        ],
        [
            (
                pl.BlockSpec((groups, tile_cols, tile_cols), lambda g: (0, g, 0)),
                sds((groups, tokens, tile_cols), BF16),
            )
        ],
        [],
        2 * tokens**3, 6 * tokens**2,
        (chan_edges, chan_edges),
    )
    tri = exchange(triangle.reshape(devices, tile_rows, tile_cols))
    d_tri, tri_t = call(
        d_tri_kernel, "d_tri", (steps,),
        [triblock, chanblock, vec, square],
        [(triblock, sds((hidden, tile_rows, tile_cols), BF16)), (chanblock, t_shape)],
        [
            pltpu.VMEM((halves, hidden * RB, 128), F32),
            pltpu.VMEM((halves, hidden * RB, 128), F32),
            pltpu.VMEM((hidden, tile_cols), F32),
        ],
        2 * positions * chans * hidden, 8 * positions * chans,
        (tri, d_proj, o_gain, w_out),
    )
    chan_d_tri = exchange(d_tri)
    update, d_gate, sum_gate, sum_out, sum_norm = call(
        update_kernel, "update", (steps,),
        [chanblock, chanblock, rowblock, vec, vec, square, vec, vec, square],
        [
            (rowblock, sds((tile_rows, tile_cols, chans), BF16)),
            (chanblock, t_shape),
            (square, sds((chans, chans), F32)),
            (square, sds((hidden, chans), F32)),
            (whole((hidden, 128)), sds((hidden, 128), F32)),
        ],
        [
            pltpu.VMEM((chans, chans), BF16),
            pltpu.VMEM((chans, hidden), BF16),
            pltpu.VMEM((4, chans, tile_cols), F32),
            pltpu.VMEM((2, hidden, tile_cols), F32),
        ],
        10 * positions * chans * hidden, 16 * positions * chans,
        (tri_t, pair_t, d_update, gain, bias, w_gate, o_gain, o_bias, w_out),
    )
    depth_rows = rows // groups
    edge_rows = pl.BlockSpec(
        (groups, depth_rows, 2, tile_rows, tile_cols), lambda s: (0, s, 0, 0, 0)
    )
    (d_chan_edges,) = call(
        d_edges_kernel, "d_edges", (groups,),
        [edge_rows, whole((groups, tokens, tile_cols))],
        [(edge_rows, sds((groups, rows, 2, tile_rows, tile_cols), BF16))],
        [],
        4 * tokens**3, 10 * tokens**2,
        (chan_edges, chan_d_tri.reshape(groups, tokens, tile_cols)),
    )
    d_edges = exchange(d_chan_edges.reshape(devices, 2, tile_rows, tile_cols))
    d_pair, sums = call(
        back_kernel, "back", (steps,),
        [edgeblock, chanblock, chanblock, maskblock, vec, vec, wide, square, square, square,
         whole((hidden, 128))],
        [
            (rowblock, sds((tile_rows, tile_cols, chans), BF16)),
            (whole((chans * 8, 128)), sds((chans * 8, 128), F32)),
        ],
        [
            pltpu.VMEM((2 * halves, hidden * RB, 128), F32),
            pltpu.VMEM((4 * hidden, chans), BF16),
            pltpu.VMEM((chans, 4 * hidden + chans), BF16),
            pltpu.VMEM((2, chans, tile_cols), F32),
            pltpu.VMEM((2, chans, tile_cols), F32),
            pltpu.VMEM((chans, 4 * hidden), F32),
        ],
        26 * positions * chans * hidden, 16 * positions * chans,
        (d_edges, pair_t, d_gate, mask_pair, gain, bias, w_in, w_gate, sum_gate, sum_out, sum_norm),
    )
    part = sds((devices, 8, 128), F32)
    arrived = exchange(sums.reshape(devices, 8, 128))
    (total,) = call(
        functools.partial(total_kernel, 1.0 / tokens), "total", (1,),
        [whole(part.shape)], [(whole(part.shape), part)], [],
        devices * 1024, devices * 8192, (arrived,),
    )
    everywhere = exchange(total).reshape(chans * 8, 128)
    small = [
        (chans, 4 * hidden), (chans, chans), (hidden, chans), (2, chans), (2, hidden),
    ]
    grads = call(
        unpack_kernel, "unpack", (1,),
        [whole((chans * 8, 128))],
        [(whole(shape), sds(shape, F32)) for shape in small],
        [], 1024, devices * 8192, (everywhere,),
    )
    return (update, d_pair, *grads)


def solution(mesh):
    return jax.shard_map(
        body,
        mesh=mesh,
        in_specs=(
            P("row", "grp", None),
            P(),
            P(),
            P(),
            P(),
            P(),
            P(),
            P(),
            P(),
            P("row", "grp", None),
        ),
        out_specs=(P("row", "grp", None), P("row", "grp", None), P(), P(), P(), P(), P()),
        check_vma=False,
    )
```

time: 870 us -> 296 us (0.34); the launches traced: 860 us -> 295 us
  local copies, waits for them, and re-layouts: 181 us -> 1.47 us
  blocking collectives: 300 us -> 137 us
  waiting for transfers between devices: 212 us -> 58 us
  Pallas kernels: 0 us -> 84.9 us
  other arithmetic: 78.7 us -> 1.38 us
  matrix products: 58 us -> 0 us
  between operations: 14.6 us -> 0.67 us
    psum x1 -> x0, waiting for transfers between devices: 133 us -> none  [body(): lax.psum((sum_in, sum_gate, sum_out, sum_in_norm, sum_out_norm), ('grp',...]
    all_to_all x5 -> x4, blocking collectives: 232 us -> 137 us  [exchange(): return lax.all_to_all(chunks, AXES, split_axis=0, concat_axis=0, tiled=True)]
    pallas_call x0 -> x9, Pallas kernels: none -> 84.9 us  [call(): pl.pallas_call(kernel, name=name, grid=grid, in_specs=ins, out_specs=[spe...]
    psum x1 -> x0, blocking collectives: 67.6 us -> none  [body(): lax.psum((sum_in, sum_gate, sum_out, sum_in_norm, sum_out_norm), ('grp',...]
    dot_general x12 -> x0, matrix products: 58 us -> none  [the longest x1 7.39 us: body(): jnp.einsum('rjc,frj->cf', normed, d_projected, preferred_element_type=jnp...]
    unnamed x42 -> x2, local copies, waits for them, and re-layouts: 45.6 us -> 1.32 us
    all_to_all x6 -> x0, local copies, waits for them, and re-layouts: 38.6 us -> none  [the longest x3 19.6 us: to_channels(): lax.all_to_all(shaped, 'grp', split_axis=1, concat_axis=5, tiled=True)]
    reshape x2 -> x0, local copies, waits for them, and re-layouts: 31.3 us -> none  [the longest x1 19.9 us: body(): projected = projected.reshape(2, 2, hidden, tile_rows, tile_cols)]
  transfers between devices with their start and end apart: 4 -> 2, of which waited for: 4 -> 2; matrix products, arithmetic and copies ran while one was open for 4% -> 0% of each run, Pallas kernels for 0% -> 8%
where the time goes in v1:
time: 296 us; the launch traced here: 295 us
  blocking collectives  137 us (46%)
  Pallas kernels  84.9 us (29%)
  waiting for transfers between devices  58 us (20%)
  starting transfers between devices  11.5 us (4%)
    all_to_all x4, blocking collectives, exchange(): return lax.all_to_all(chunks, AXES, split_axis=0, concat_axis=0, tiled=True)  137 us
    pallas_call x9, Pallas kernels, call(): pl.pallas_call(kernel, name=name, grid=grid, in_specs=ins, out_specs=[spe...  84.9 us
    all_to_all x2, waiting for transfers between devices, exchange(): return lax.all_to_all(chunks, AXES, split_axis=0, concat_axis=0, tiled=True)  58 us
    all_to_all x2, starting transfers between devices, exchange(): return lax.all_to_all(chunks, AXES, split_axis=0, concat_axis=0, tiled=True)  11.5 us
  transfers between devices with their start and end apart: 2, of which 2 were waited for; matrix products, arithmetic and copies ran while one was open for 0% of the time, Pallas kernels for 8%

profile of v1, /device:TPU:1, one launch (start us, length us, event | category | flops | bytes accessed | tf_op | source)
XLA Modules:
  0.0 294.8 jit_solution(14244830496344260799)
XLA Ops:
  0.6 0.7 convert_element_type.3
  1.3 0.1 dynamic_slice.6
  1.4 0.1 dynamic_slice.7
  1.5 0.7 broadcast_multiply_fusion.mask
  2.2 12.6 %edges.1 = (bf16[128,2,32,256]{3,2,1,0:T(8,128)(2,1)}, bf16[32,128,256]{2,1,0:T(8,128)(2,1)}) custom-call(bf16[32,256,128]{2,1,0:T(8,128)(2,1)} %pair.1, f32[32,256]{1,0:T(8,128)} %broadcast_multiply_fusion.mask, f32[1,128]{1,0:T(1,128)} %bitcast.20, f32[1,128]{1,0:T(1,128)} %bitcast.24, bf16[128,512]{1,0:T(8,128)(2,1)} %w_in.3), custom_call_target="tpu_custom_call" | custom-call | flops 1073741824 | bytes 16777216 | tf_op jit(solution)/shard_map/edges/pallas_call | solution.py:62
  14.8 63.1 %all_to_all.30 = bf16[128,2,32,256]{3,2,1,0:T(8,128)(2,1)} all-to-all(bf16[128,2,32,256]{3,2,1,0:T(8,128)(2,1)} %get-tuple-element.23), channel_id=1, replica_groups=mesh['grp'=4,'row'=32] {'grp','row'}, dimensions={0} | all-to-all | bytes 8388608 | tf_op jit(solution)/shard_map/all_to_all | solution.py:308
  77.8 6.1 %triangle.1 = bf16[4,1024,256]{2,1,0:T(8,128)(2,1)} custom-call(bf16[4,32,2,32,256]{4,3,2,1,0:T(8,128)(2,1)} %bitcast.10, bf16[4,32,2,32,256]{4,3,2,1,0:T(8,128)(2,1)} %bitcast.11), custom_call_target="tpu_custom_call" | custom-call | flops 2147483648 | bytes 6291456 | tf_op jit(solution)/shard_map/triangle/pallas_call | solution.py:62
  83.9 5.5 %all-to-all-start.1 = ((bf16[128,32,256]{2,1,0:T(8,128)(2,1)}), bf16[128,32,256]{2,1,0:T(8,128)(2,1)S(1)}, u32[]{:S(2)}, u32[]{:S(2)}) async-start(bf16[128,32,256]{2,1,0:T(8,128)(2,1)} %bitcast.13), calls=%async_computation.1 | async-start | bytes 4194304 | tf_op jit(solution)/shard_map/all_to_all | solution.py:308
  89.4 7.2 %cotangent.1.d_proj = bf16[32,128,256]{2,1,0:T(8,128)(2,1)} custom-call(bf16[32,128,256]{2,1,0:T(8,128)(2,1)} %get-tuple-element.24.pair_t, bf16[32,256,128]{2,1,0:T(8,128)(2,1)} %d_update.3, f32[1,128]{1,0:T(1,128)} %bitcast.21, f32[1,128]{1,0:T(1,128)} %bitcast.25, bf16[128,128]{1,0:T(8,128)(2,1)} %w_gate.5), custom_call_target="tpu_custom_call" | custom-call | flops 268435456 | bytes 8388608 | tf_op jit(solution)/shard_map/cotangent/pallas_call | solution.py:62
  96.7 22.1 %all-to-all-done.1.tri = bf16[128,32,256]{2,1,0:T(8,128)(2,1)S(1)} async-done(((bf16[128,32,256]{2,1,0:T(8,128)(2,1)}), bf16[128,32,256]{2,1,0:T(8,128)(2,1)S(1)}, u32[]{:S(2)}, u32[]{:S(2)}) %all-to-all-start.1) | async-done | bytes 2097184 | tf_op jit(solution)/shard_map/all_to_all | solution.py:308
  118.8 0.0 copy-start
  118.8 1.3 copy-done
  120.1 9.8 %d_tri.1 = (bf16[128,32,256]{2,1,0:T(8,128)(2,1)}, bf16[32,128,256]{2,1,0:T(8,128)(2,1)}) custom-call(bf16[128,32,256]{2,1,0:T(8,128)(2,1)} %copy-done, bf16[32,128,256]{2,1,0:T(8,128)(2,1)} %cotangent.1.d_proj, f32[1,128]{1,0:T(1,128)} %bitcast.18, bf16[128,128]{1,0:T(8,128)(2,1)} %w_out.3), custom_call_target="tpu_custom_call" | custom-call | flops 268435456 | bytes 8388608 | tf_op jit(solution)/shard_map/d_tri/pallas_call | solution.py:62
  129.9 35.3 %all_to_all.31 = bf16[128,32,256]{2,1,0:T(8,128)(2,1)} all-to-all(bf16[128,32,256]{2,1,0:T(8,128)(2,1)} %get-tuple-element.27), channel_id=1, replica_groups=mesh['grp'=4,'row'=32] {'grp','row'}, dimensions={0} | all-to-all | bytes 4194304 | tf_op jit(solution)/shard_map/all_to_all | solution.py:308
  165.2 8.4 %d_edges.1 = bf16[4,32,2,32,256]{4,3,2,1,0:T(8,128)(2,1)} custom-call(bf16[4,32,2,32,256]{4,3,2,1,0:T(8,128)(2,1)} %bitcast.12, bf16[4,1024,256]{2,1,0:T(8,128)(2,1)} %bitcast.15), custom_call_target="tpu_custom_call" | custom-call | flops 4294967296 | bytes 10485760 | tf_op jit(solution)/shard_map/d_edges/pallas_call | solution.py:62
  173.7 6.0 %all-to-all-start.3 = ((bf16[128,2,32,256]{3,2,1,0:T(8,128)(2,1)}), bf16[128,2,32,256]{3,2,1,0:T(8,128)(2,1)}, u32[]{:S(2)}, u32[]{:S(2)}) async-start(bf16[128,2,32,256]{3,2,1,0:T(8,128)(2,1)} %bitcast.14), calls=%async_computation.3 | async-start | bytes 8388608 | tf_op jit(solution)/shard_map/all_to_all | solution.py:308
  179.7 15.4 %update.1 = (bf16[32,256,128]{2,1,0:T(8,128)(2,1)}, bf16[32,128,256]{2,1,0:T(8,128)(2,1)}, f32[128,128]{1,0:T(8,128)}, f32[128,128]{1,0:T(8,128)}, f32[128,128]{1,0:T(8,128)}) custom-call(bf16[32,128,256]{2,1,0:T(8,128)(2,1)} %get-tuple-element.25.tri_t, bf16[32,128,256]{2,1,0:T(8,128)(2,1)} %get-tuple-element.24.pair_t, bf16[32,256,128]{2,1,0:T(8,128)(2,1)} %d_update.3, ...), custom_call_target="tpu_custom_call" | custom-call | flops 1342177280 | bytes 16777216 | tf_op jit(solution)/shard_map/update/pallas_call | solution.py:62
  195.0 35.8 %all-to-all-done.3.d_edges = bf16[128,2,32,256]{3,2,1,0:T(8,128)(2,1)} async-done(((bf16[128,2,32,256]{3,2,1,0:T(8,128)(2,1)}), bf16[128,2,32,256]{3,2,1,0:T(8,128)(2,1)}, u32[]{:S(2)}, u32[]{:S(2)}) %all-to-all-start.3) | async-done | bytes 4194336 | tf_op jit(solution)/shard_map/all_to_all | solution.py:308
  230.9 21.5 %back.1 = (bf16[32,256,128]{2,1,0:T(8,128)(2,1)}, f32[1024,128]{1,0:T(8,128)}) custom-call(bf16[128,2,32,256]{3,2,1,0:T(8,128)(2,1)} %all-to-all-done.3.d_edges, bf16[32,128,256]{2,1,0:T(8,128)(2,1)} %get-tuple-element.24.pair_t, bf16[32,128,256]{2,1,0:T(8,128)(2,1)} %get-tuple-element.28.d_gate, f32[32,256]{1,0:T(8,128)} %broadcast_multiply_fusion.mask, ...), custom_call_target="tpu_custom_call" | custom-call | flops 3489660928 | bytes 16777216 | tf_op jit(solution)/shard_map/back/pallas_call | solution.py:62
  252.4 19.5 %all_to_all.32.arrived = f32[128,8,128]{2,1,0:T(8,128)} all-to-all(f32[128,8,128]{2,1,0:T(8,128)} %bitcast.17), channel_id=1, replica_groups=mesh['grp'=4,'row'=32] {'grp','row'}, dimensions={0} | all-to-all | bytes 1048576 | tf_op jit(solution)/shard_map/all_to_all | solution.py:308
  271.9 2.0 total.1
  273.9 19.1 %all_to_all.33 = f32[128,8,128]{2,1,0:T(8,128)} all-to-all(f32[128,8,128]{2,1,0:T(8,128)} %total.1), channel_id=1, replica_groups=mesh['grp'=4,'row'=32] {'grp','row'}, dimensions={0} | all-to-all | bytes 1048576 | tf_op jit(solution)/shard_map/all_to_all | solution.py:308
  293.0 1.8 unpack.1
Async XLA Ops:
  83.9 34.8 %all-to-all-start.1 = ((bf16[128,32,256]{2,1,0:T(8,128)(2,1)}), bf16[128,32,256]{2,1,0:T(8,128)(2,1)S(1)}, u32[]{:S(2)}, u32[]{:S(2)}) async-start(bf16[128,32,256]{2,1,0:T(8,128)(2,1)} %bitcast.13), calls=%async_computation.1 | async-start | bytes 4194304 | tf_op jit(solution)/shard_map/all_to_all | solution.py:308
  118.8 1.3 copy-start
  173.7 57.2 %all-to-all-start.3 = ((bf16[128,2,32,256]{3,2,1,0:T(8,128)(2,1)}), bf16[128,2,32,256]{3,2,1,0:T(8,128)(2,1)}, u32[]{:S(2)}, u32[]{:S(2)}) async-start(bf16[128,2,32,256]{3,2,1,0:T(8,128)(2,1)} %bitcast.14), calls=%async_computation.3 | async-start | bytes 8388608 | tf_op jit(solution)/shard_map/all_to_all | solution.py:308

commit v2 on v1

--- a/solution.py
+++ b/solution.py
@@ -10,6 +10,8 @@
 EPS = 1e-05
 AXES = ("grp", "row")
 RB = 16
+BATCH = 4
+VMEM_LIMIT = 28 * 1024 * 1024
 F32 = jnp.float32
 BF16 = jnp.bfloat16
 
@@ -46,19 +48,21 @@
     )
 
 
-def put_rows(scratch, slot, r, values):
-    chans, width = values.shape
-    for h in range(width // 128):
-        scratch[slot + h, pl.ds(r, chans, stride=RB), :] = values[:, h * 128 : (h + 1) * 128]
-
-
-def get_rows(scratch, slot, r, chans, width):
-    return jnp.concatenate(
-        [scratch[slot + h, pl.ds(r, chans, stride=RB), :] for h in range(width // 128)], axis=1
-    )
-
-
-def call(kernel, name, grid, ins, outs, scratch, flops, nbytes, args):
+def fold(values):
+    return sum(values[:, i : i + 128] for i in range(0, values.shape[1], 128))
+
+
+def swap_rows(values):
+    return jnp.swapaxes(values, 0, 1)
+
+
+def call(kernel, name, grid, ins, outs, scratch, flops, nbytes, args, in_hbm=None):
+    if in_hbm is None:
+        in_hbm = range(len(args))
+    args = [
+        pltpu.with_memory_space_constraint(arg, pltpu.HBM) if i in in_hbm else arg
+        for i, arg in enumerate(args)
+    ]
     return pl.pallas_call(
         kernel,
         name=name,
@@ -67,7 +71,7 @@
         out_specs=[spec for spec, _ in outs],
         out_shape=[shape for _, shape in outs],
         scratch_shapes=scratch,
-        compiler_params=pltpu.CompilerParams(vmem_limit_bytes=60 * 1024 * 1024),
+        compiler_params=pltpu.CompilerParams(vmem_limit_bytes=VMEM_LIMIT),
         cost_estimate=pl.CostEstimate(flops=flops, bytes_accessed=nbytes, transcendentals=0),
     )(*args)
 
@@ -76,10 +80,16 @@
     return pl.BlockSpec(shape, lambda *_: (0,) * len(shape))
 
 
-def edges_kernel(pair, mask, gain, bias, w_in, edges, pair_t, scr, w_t, cols):
-    chans = pair.shape[2]
+def edges_kernel(
+    pair, row_tokens, col_tokens, gain, bias, w_in, edges, pair_t, mask, w_t, cols
+):
     width = pair.shape[1]
     hidden = edges.shape[0]
+    first_row = (lax.axis_index("row") * pl.num_programs(0) + pl.program_id(0)) * RB
+    first_col = lax.axis_index("grp") * (width // 128)
+    col_mask = jnp.concatenate(
+        [col_tokens[pl.ds(first_col + i, 1), :] for i in range(width // 128)], axis=1
+    ).astype(F32)
 
     @pl.when(pl.program_id(0) == 0)
     def _():
@@ -87,25 +97,21 @@
         cols[0] = columns(gain[...], width)
         cols[1] = columns(bias[...], width)
 
-    def step(r, carry):
+    sides = [[], []]
+    for r in range(RB):
         x_t = pair[r].T
         pair_t[r] = x_t
         hat, _ = norm0(x_t.astype(F32))
         normed = (hat * cols[0] + cols[1]).astype(BF16)
         proj = dot(w_t[...], normed)
-        m = mask[pl.ds(r, 1), :]
+        m = col_mask * row_tokens[first_row + r].astype(F32)
+        mask[r : r + 1, :] = m
         for side in range(2):
             gate = sigmoid(proj[side * 2 * hidden : (side * 2 + 1) * hidden])
             value = proj[(side * 2 + 1) * hidden : (side * 2 + 2) * hidden]
-            put_rows(scr, side * (width // 128), r, gate * value * m)
-        return carry
-
-    lax.fori_loop(0, RB, step, 0, unroll=2)
+            sides[side].append((gate * value * m).astype(BF16))
     for side in range(2):
-        for h in range(width // 128):
-            edges[:, side, :, h * 128 : (h + 1) * 128] = (
-                scr[side * (width // 128) + h].reshape(hidden, RB, 128).astype(BF16)
-            )
+        edges[:, side] = swap_rows(jnp.stack(sides[side]))
 
 
 def cotangent_kernel(pair_t, d_update, gain, bias, w_gate, d_proj, wg_t, cols):
@@ -117,14 +123,11 @@
         cols[0] = columns(gain[...], width)
         cols[1] = columns(bias[...], width)
 
-    def step(r, carry):
+    for r in range(RB):
         hat, _ = norm0(pair_t[r].astype(F32))
         normed = (hat * cols[0] + cols[1]).astype(BF16)
         gate = sigmoid(dot(wg_t[...], normed))
         d_proj[r] = (d_update[r].T.astype(F32) * gate).astype(BF16)
-        return carry
-
-    lax.fori_loop(0, RB, step, 0, unroll=2)
 
 
 def triangle_kernel(left, right, out):
@@ -135,30 +138,21 @@
         out[h] = dot(left_t, right[h].reshape(depth, width)).astype(BF16)
 
 
-def d_tri_kernel(tri, d_proj, gain, w_out, d_tri, tri_t, scr_in, scr_out, cols):
-    hidden, _, width = tri.shape
-    halves = width // 128
+def d_tri_kernel(tri, d_proj, gain, w_out, d_tri, tri_t, cols):
+    width = tri.shape[2]
 
     @pl.when(pl.program_id(0) == 0)
     def _():
         cols[...] = columns(gain[...], width)
 
-    for h in range(halves):
-        scr_in[h] = tri[:, :, h * 128 : (h + 1) * 128].astype(F32).reshape(hidden * RB, 128)
-
-    def step(r, carry):
-        t = get_rows(scr_in, 0, r, hidden, width)
-        tri_t[r] = t.astype(BF16)
-        hat, inv = norm0(t)
+    arrived = swap_rows(tri[...])
+    tri_t[...] = arrived
+    grads = []
+    for r in range(RB):
+        hat, inv = norm0(arrived[r].astype(F32))
         grad = dot(w_out[...], d_proj[r]) * cols[...]
-        put_rows(scr_out, 0, r, norm0_back(grad, hat, inv))
-        return carry
-
-    lax.fori_loop(0, RB, step, 0, unroll=2)
-    for h in range(halves):
-        d_tri[:, :, h * 128 : (h + 1) * 128] = (
-            scr_out[h].reshape(hidden, RB, 128).astype(BF16)
-        )
+        grads.append(norm0_back(grad, hat, inv).astype(BF16))
+    d_tri[...] = swap_rows(jnp.stack(grads))
 
 
 def update_kernel(
@@ -195,11 +189,11 @@
         sum_out[...] += dot_nt(tri_norm, d_proj)
         sum_gate[...] += dot_nt(normed, d_gate_pre)
         d_tri_norm = dot(w_out[...], d_proj)
-        acc[0] += d_tri_norm * tri_hat
-        acc[1] += d_tri_norm
+        acc[0] += fold(d_tri_norm * tri_hat)
+        acc[1] += fold(d_tri_norm)
         return carry
 
-    lax.fori_loop(0, RB, step, 0, unroll=2)
+    lax.fori_loop(0, RB, step, 0, unroll=4)
 
     @pl.when(pl.program_id(0) == pl.num_programs(0) - 1)
     def _():
@@ -229,11 +223,10 @@
 def back_kernel(
     d_edges, pair_t, d_gate, mask, gain, bias, w_in, w_gate, sum_gate, sum_out, sum_norm,
     d_pair, sums,
-    scr, w_t, w_all, cols, acc, acc_in,
+    w_t, w_all, cols, acc, acc_in,
 ):
     hidden = d_edges.shape[0]
     chans, width = pair_t.shape[1:]
-    halves = width // 128
 
     @pl.when(pl.program_id(0) == 0)
     def _():
@@ -245,33 +238,29 @@
         acc[...] = jnp.zeros_like(acc)
         acc_in[...] = jnp.zeros_like(acc_in)
 
-    for side in range(2):
-        for h in range(halves):
-            scr[side * halves + h] = (
-                d_edges[:, side, :, h * 128 : (h + 1) * 128].astype(F32).reshape(hidden * RB, 128)
-            )
-
-    def step(r, carry):
-        hat, inv = norm0(pair_t[r].astype(F32))
-        normed = (hat * cols[0] + cols[1]).astype(BF16)
-        proj = dot(w_t[...], normed)
-        m = mask[pl.ds(r, 1), :]
-        parts = []
-        for side in range(2):
-            gate = sigmoid(proj[side * 2 * hidden : (side * 2 + 1) * hidden])
-            value = proj[(side * 2 + 1) * hidden : (side * 2 + 2) * hidden]
-            d_value = get_rows(scr, side * halves, r, hidden, width) * m * gate
-            parts.append((d_value * value * (1.0 - gate)).astype(BF16))
-            parts.append(d_value.astype(BF16))
-        d_projected = jnp.concatenate(parts, axis=0)
-        acc_in[...] += dot_nt(normed, d_projected)
-        d_normed = dot(w_all[...], jnp.concatenate([d_projected, d_gate[r]], axis=0))
-        acc[0] += d_normed * hat
-        acc[1] += d_normed
-        d_pair[r] = norm0_back(d_normed * cols[0], hat, inv).astype(BF16).T
-        return carry
-
-    lax.fori_loop(0, RB, step, 0, unroll=2)
+    arrived = [swap_rows(d_edges[:, side]) for side in range(2)]
+    for first_row in range(0, RB, BATCH):
+        left, right = [], []
+        for r in range(first_row, first_row + BATCH):
+            hat, inv = norm0(pair_t[r].astype(F32))
+            normed = (hat * cols[0] + cols[1]).astype(BF16)
+            proj = dot(w_t[...], normed)
+            m = mask[r : r + 1, :]
+            parts = []
+            for side in range(2):
+                gate = sigmoid(proj[side * 2 * hidden : (side * 2 + 1) * hidden])
+                value = proj[(side * 2 + 1) * hidden : (side * 2 + 2) * hidden]
+                d_value = arrived[side][r].astype(F32) * m * gate
+                parts.append((d_value * value * (1.0 - gate)).astype(BF16))
+                parts.append(d_value.astype(BF16))
+            d_projected = jnp.concatenate(parts, axis=0)
+            left.append(normed)
+            right.append(d_projected)
+            d_normed = dot(w_all[...], jnp.concatenate([d_projected, d_gate[r]], axis=0))
+            acc[0] += fold(d_normed * hat)
+            acc[1] += fold(d_normed)
+            d_pair[r] = norm0_back(d_normed * cols[0], hat, inv).astype(BF16).T
+        acc_in[...] += dot_nt(jnp.concatenate(left, axis=1), jnp.concatenate(right, axis=1))
 
     @pl.when(pl.program_id(0) == pl.num_programs(0) - 1)
     def _():
@@ -316,14 +305,9 @@
     tokens = token_mask.shape[0]
     devices = groups * rows
     steps = tile_rows // RB
-    halves = tile_cols // 128
     positions = tile_rows * tile_cols
     sds = jax.ShapeDtypeStruct
 
-    mask_all = token_mask.astype(F32)
-    row_mask = lax.dynamic_slice_in_dim(mask_all, lax.axis_index("row") * tile_rows, tile_rows)
-    col_mask = lax.dynamic_slice_in_dim(mask_all, lax.axis_index("grp") * tile_cols, tile_cols)
-    mask_pair = row_mask[:, None] * col_mask[None, :]
     gain, bias = in_gain[None], in_bias[None]
     o_gain, o_bias = out_gain[None], out_bias[None]
 
@@ -337,23 +321,30 @@
     triblock = pl.BlockSpec((hidden, RB, tile_cols), lambda s: (0, s, 0))
     t_shape = sds((tile_rows, chans, tile_cols), BF16)
 
-    edges, pair_t = call(
+    edges, pair_t, mask_pair = call(
         edges_kernel, "edges", (steps,),
-        [rowblock, maskblock, vec, vec, wide],
-        [(edgeblock, sds((hidden, 2, tile_rows, tile_cols), BF16)), (chanblock, t_shape)],
-        [
-            pltpu.VMEM((2 * halves, hidden * RB, 128), F32),
+        [
+            rowblock, pl.BlockSpec(memory_space=pltpu.SMEM), whole((tokens // 128, 128)),
+            vec, vec, wide,
+        ],
+        [
+            (edgeblock, sds((hidden, 2, tile_rows, tile_cols), BF16)),
+            (chanblock, t_shape),
+            (maskblock, sds((tile_rows, tile_cols), F32)),
+        ],
+        [
             pltpu.VMEM((4 * hidden, chans), BF16),
             pltpu.VMEM((2, chans, tile_cols), F32),
         ],
         2 * positions * chans * 4 * hidden, 16 * positions * chans,
-        (pair, mask_pair, gain, bias, w_in),
+        (pair, token_mask, token_mask.reshape(tokens // 128, 128), gain, bias, w_in),
+        in_hbm=(0, 2, 3, 4, 5),
     )
     chan_edges = exchange(edges)
     (d_proj,) = call(
         cotangent_kernel, "cotangent", (steps,),
         [chanblock, rowblock, vec, vec, square],
-        [(chanblock, t_shape)],
+        [(chanblock, pltpu.HBM(t_shape.shape, BF16))],
         [pltpu.VMEM((chans, hidden), BF16), pltpu.VMEM((2, chans, tile_cols), F32)],
         2 * positions * chans * hidden, 8 * positions * chans,
         (pair_t, d_update, gain, bias, w_gate),
@@ -374,19 +365,22 @@
         [],
         2 * tokens**3, 6 * tokens**2,
         (chan_edges, chan_edges),
+        in_hbm=(),
     )
     tri = exchange(triangle.reshape(devices, tile_rows, tile_cols))
     d_tri, tri_t = call(
         d_tri_kernel, "d_tri", (steps,),
         [triblock, chanblock, vec, square],
-        [(triblock, sds((hidden, tile_rows, tile_cols), BF16)), (chanblock, t_shape)],
-        [
-            pltpu.VMEM((halves, hidden * RB, 128), F32),
-            pltpu.VMEM((halves, hidden * RB, 128), F32),
+        [
+            (triblock, sds((hidden, tile_rows, tile_cols), BF16)),
+            (chanblock, pltpu.HBM(t_shape.shape, BF16)),
+        ],
+        [
             pltpu.VMEM((hidden, tile_cols), F32),
         ],
         2 * positions * chans * hidden, 8 * positions * chans,
         (tri, d_proj, o_gain, w_out),
+        in_hbm=(1, 2, 3),
     )
     chan_d_tri = exchange(d_tri)
     update, d_gate, sum_gate, sum_out, sum_norm = call(
@@ -394,7 +388,7 @@
         [chanblock, chanblock, rowblock, vec, vec, square, vec, vec, square],
         [
             (rowblock, sds((tile_rows, tile_cols, chans), BF16)),
-            (chanblock, t_shape),
+            (chanblock, pltpu.HBM(t_shape.shape, BF16)),
             (square, sds((chans, chans), F32)),
             (square, sds((hidden, chans), F32)),
             (whole((hidden, 128)), sds((hidden, 128), F32)),
@@ -403,7 +397,7 @@
             pltpu.VMEM((chans, chans), BF16),
             pltpu.VMEM((chans, hidden), BF16),
             pltpu.VMEM((4, chans, tile_cols), F32),
-            pltpu.VMEM((2, hidden, tile_cols), F32),
+            pltpu.VMEM((2, hidden, 128), F32),
         ],
         10 * positions * chans * hidden, 16 * positions * chans,
         (tri_t, pair_t, d_update, gain, bias, w_gate, o_gain, o_bias, w_out),
@@ -415,10 +409,11 @@
     (d_chan_edges,) = call(
         d_edges_kernel, "d_edges", (groups,),
         [edge_rows, whole((groups, tokens, tile_cols))],
-        [(edge_rows, sds((groups, rows, 2, tile_rows, tile_cols), BF16))],
+        [(edge_rows, pltpu.HBM((groups, rows, 2, tile_rows, tile_cols), BF16))],
         [],
         4 * tokens**3, 10 * tokens**2,
         (chan_edges, chan_d_tri.reshape(groups, tokens, tile_cols)),
+        in_hbm=(),
     )
     d_edges = exchange(d_chan_edges.reshape(devices, 2, tile_rows, tile_cols))
     d_pair, sums = call(
@@ -430,15 +425,15 @@
             (whole((chans * 8, 128)), sds((chans * 8, 128), F32)),
         ],
         [
-            pltpu.VMEM((2 * halves, hidden * RB, 128), F32),
             pltpu.VMEM((4 * hidden, chans), BF16),
             pltpu.VMEM((chans, 4 * hidden + chans), BF16),
             pltpu.VMEM((2, chans, tile_cols), F32),
-            pltpu.VMEM((2, chans, tile_cols), F32),
+            pltpu.VMEM((2, chans, 128), F32),
             pltpu.VMEM((chans, 4 * hidden), F32),
         ],
         26 * positions * chans * hidden, 16 * positions * chans,
         (d_edges, pair_t, d_gate, mask_pair, gain, bias, w_in, w_gate, sum_gate, sum_out, sum_norm),
+        in_hbm=(0, 1, 2, 4, 5, 6, 7),
     )
     part = sds((devices, 8, 128), F32)
     arrived = exchange(sums.reshape(devices, 8, 128))
@@ -446,6 +441,7 @@
         functools.partial(total_kernel, 1.0 / tokens), "total", (1,),
         [whole(part.shape)], [(whole(part.shape), part)], [],
         devices * 1024, devices * 8192, (arrived,),
+        in_hbm=(),
     )
     everywhere = exchange(total).reshape(chans * 8, 128)
     small = [
@@ -456,6 +452,7 @@
         [whole((chans * 8, 128))],
         [(whole(shape), sds(shape, F32)) for shape in small],
         [], 1024, devices * 8192, (everywhere,),
+        in_hbm=(),
     )
     return (update, d_pair, *grads)
 

time: 296 us -> 268 us (0.905)
  Pallas kernels: 84.9 us -> 60.5 us
  waiting for transfers between devices: 58 us -> 61.7 us
  blocking collectives: 137 us -> 134 us
    pallas_call x9, Pallas kernels: 84.9 us -> 60.5 us  [call(): pl.pallas_call(kernel, name=name, grid=grid, in_specs=ins, out_specs=[spe...]
    all_to_all x2, waiting for transfers between devices: 58 us -> 61.7 us  [exchange(): return lax.all_to_all(chunks, AXES, split_axis=0, concat_axis=0, tiled=True)]
    all_to_all x4, blocking collectives: 137 us -> 134 us  [exchange(): return lax.all_to_all(chunks, AXES, split_axis=0, concat_axis=0, tiled=True)]
  transfers between devices with their start and end apart: 2 -> 2, of which waited for: 2 -> 2; matrix products, arithmetic and copies ran while one was open for 0% -> 0% of each run, Pallas kernels for 8% -> 7%
where the time goes in v2:
time: 268 us
  blocking collectives  134 us (50%)
  waiting for transfers between devices  61.7 us (23%)
  Pallas kernels  60.5 us (23%)
  starting transfers between devices  11.5 us (4%)
    all_to_all x4, blocking collectives, exchange(): return lax.all_to_all(chunks, AXES, split_axis=0, concat_axis=0, tiled=True)  134 us
    all_to_all x2, waiting for transfers between devices, exchange(): return lax.all_to_all(chunks, AXES, split_axis=0, concat_axis=0, tiled=True)  61.7 us
    pallas_call x9, Pallas kernels, call(): pl.pallas_call(kernel, name=name, grid=grid, in_specs=ins, out_specs=[spe...  60.5 us
    all_to_all x2, starting transfers between devices, exchange(): return lax.all_to_all(chunks, AXES, split_axis=0, concat_axis=0, tiled=True)  11.5 us
  transfers between devices with their start and end apart: 2, of which 2 were waited for; matrix products, arithmetic and copies ran while one was open for 0% of the time, Pallas kernels for 7%

profile of v2, /device:TPU:1, one launch (start us, length us, event | category | flops | bytes accessed | tf_op | source)
XLA Modules:
  0.0 268.1 jit_solution(4510487459443905543)
XLA Ops:
  0.6 6.8 %edges.1 = (bf16[128,2,32,256]{3,2,1,0:T(8,128)(2,1)S(1)}, bf16[32,128,256]{2,1,0:T(8,128)(2,1)S(1)}, f32[32,256]{1,0:T(8,128)S(1)}) custom-call(bf16[32,256,128]{2,1,0:T(8,128)(2,1)} %pair.1, s32[1024]{0:T(1024)} %row_tokens.1, s32[8,128]{1,0:T(8,128)} %bitcast.29, f32[1,128]{1,0:T(1,128)} %bitcast.20, f32[1,128]{1,0:T(1,128)} %bitcast.24, ...), custom_call_target="tpu_custom_call" | custom-call | flops 1073741824 | bytes 16777216 | tf_op jit(solution)/shard_map/edges/pallas_call | solution.py:66
  7.4 0.0 copy-start.2
  7.4 62.7 %all_to_all.30 = bf16[128,2,32,256]{3,2,1,0:T(8,128)(2,1)S(1)} all-to-all(bf16[128,2,32,256]{3,2,1,0:T(8,128)(2,1)S(1)} %get-tuple-element.24), channel_id=1, replica_groups=mesh['grp'=4,'row'=32] {'grp','row'}, dimensions={0} | all-to-all | bytes 8388608 | tf_op jit(solution)/shard_map/all_to_all | solution.py:297
  70.2 0.0 copy-done.2
  70.2 0.0 copy-start
  70.2 4.5 %triangle.1 = bf16[4,1024,256]{2,1,0:T(8,128)(2,1)} custom-call(bf16[4,32,2,32,256]{4,3,2,1,0:T(8,128)(2,1)S(1)} %bitcast.11, bf16[4,32,2,32,256]{4,3,2,1,0:T(8,128)(2,1)S(1)} %bitcast.12), custom_call_target="tpu_custom_call" | custom-call | flops 2147483648 | bytes 6291456 | tf_op jit(solution)/shard_map/triangle/pallas_call | solution.py:66
  74.7 0.0 copy-done
  74.7 5.5 %all-to-all-start.1 = ((bf16[128,32,256]{2,1,0:T(8,128)(2,1)}), bf16[128,32,256]{2,1,0:T(8,128)(2,1)S(1)}, u32[]{:S(2)}, u32[]{:S(2)}) async-start(bf16[128,32,256]{2,1,0:T(8,128)(2,1)} %bitcast.4), calls=%async_computation.1 | async-start | bytes 4194304 | tf_op jit(solution)/shard_map/all_to_all | solution.py:297
  80.2 5.2 %cotangent.1.d_proj = bf16[32,128,256]{2,1,0:T(8,128)(2,1)} custom-call(bf16[32,128,256]{2,1,0:T(8,128)(2,1)} %copy-done.2, bf16[32,256,128]{2,1,0:T(8,128)(2,1)} %d_update.3, f32[1,128]{1,0:T(1,128)} %bitcast.21, f32[1,128]{1,0:T(1,128)} %bitcast.25, bf16[128,128]{1,0:T(8,128)(2,1)} %w_gate.5), custom_call_target="tpu_custom_call" | custom-call | flops 268435456 | bytes 8388608 | tf_op jit(solution)/shard_map/cotangent/pallas_call | solution.py:66
  85.4 24.1 %all-to-all-done.1.tri = bf16[128,32,256]{2,1,0:T(8,128)(2,1)S(1)} async-done(((bf16[128,32,256]{2,1,0:T(8,128)(2,1)}), bf16[128,32,256]{2,1,0:T(8,128)(2,1)S(1)}, u32[]{:S(2)}, u32[]{:S(2)}) %all-to-all-start.1) | async-done | bytes 2097184 | tf_op jit(solution)/shard_map/all_to_all | solution.py:297
  109.6 6.7 %d_tri.1 = (bf16[128,32,256]{2,1,0:T(8,128)(2,1)S(1)}, bf16[32,128,256]{2,1,0:T(8,128)(2,1)}) custom-call(bf16[128,32,256]{2,1,0:T(8,128)(2,1)S(1)} %all-to-all-done.1.tri, bf16[32,128,256]{2,1,0:T(8,128)(2,1)} %cotangent.1.d_proj, f32[1,128]{1,0:T(1,128)} %bitcast.18, bf16[128,128]{1,0:T(8,128)(2,1)} %w_out.3), custom_call_target="tpu_custom_call" | custom-call | flops 268435456 | bytes 8388608 | tf_op jit(solution)/shard_map/d_tri/pallas_call | solution.py:66
  116.2 0.0 copy-start.1
  116.2 34.3 %all_to_all.31 = bf16[128,32,256]{2,1,0:T(8,128)(2,1)S(1)} all-to-all(bf16[128,32,256]{2,1,0:T(8,128)(2,1)S(1)} %get-tuple-element.28), channel_id=1, replica_groups=mesh['grp'=4,'row'=32] {'grp','row'}, dimensions={0} | all-to-all | bytes 4194304 | tf_op jit(solution)/shard_map/all_to_all | solution.py:297
  150.5 0.0 copy-done.1
  150.5 6.4 %d_edges.1 = bf16[4,32,2,32,256]{4,3,2,1,0:T(8,128)(2,1)} custom-call(bf16[4,32,2,32,256]{4,3,2,1,0:T(8,128)(2,1)S(1)} %bitcast.13, bf16[4,1024,256]{2,1,0:T(8,128)(2,1)S(1)} %bitcast.14), custom_call_target="tpu_custom_call" | custom-call | flops 4294967296 | bytes 10485760 | tf_op jit(solution)/shard_map/d_edges/pallas_call | solution.py:66
  156.9 6.0 %all-to-all-start.3 = ((bf16[128,2,32,256]{3,2,1,0:T(8,128)(2,1)}), bf16[128,2,32,256]{3,2,1,0:T(8,128)(2,1)}, u32[]{:S(2)}, u32[]{:S(2)}) async-start(bf16[128,2,32,256]{3,2,1,0:T(8,128)(2,1)} %bitcast.17), calls=%async_computation.3 | async-start | bytes 8388608 | tf_op jit(solution)/shard_map/all_to_all | solution.py:297
  162.9 13.7 %update.1 = (bf16[32,256,128]{2,1,0:T(8,128)(2,1)}, bf16[32,128,256]{2,1,0:T(8,128)(2,1)}, f32[128,128]{1,0:T(8,128)S(1)}, f32[128,128]{1,0:T(8,128)S(1)}, f32[128,128]{1,0:T(8,128)S(1)}) custom-call(bf16[32,128,256]{2,1,0:T(8,128)(2,1)} %get-tuple-element.26.tri_t, bf16[32,128,256]{2,1,0:T(8,128)(2,1)} %copy-done.2, bf16[32,256,128]{2,1,0:T(8,128)(2,1)} %d_update.3, ...), custom_call_target="tpu_custom_call" | custom-call | flops 1342177280 | bytes 16777216 | tf_op jit(solution)/shard_map/update/pallas_call | solution.py:66
  176.6 37.5 %all-to-all-done.3.d_edges = bf16[128,2,32,256]{3,2,1,0:T(8,128)(2,1)} async-done(((bf16[128,2,32,256]{3,2,1,0:T(8,128)(2,1)}), bf16[128,2,32,256]{3,2,1,0:T(8,128)(2,1)}, u32[]{:S(2)}, u32[]{:S(2)}) %all-to-all-start.3) | async-done | bytes 4194336 | tf_op jit(solution)/shard_map/all_to_all | solution.py:297
  214.1 16.3 %back.1 = (bf16[32,256,128]{2,1,0:T(8,128)(2,1)}, f32[1024,128]{1,0:T(8,128)S(1)}) custom-call(bf16[128,2,32,256]{3,2,1,0:T(8,128)(2,1)} %all-to-all-done.3.d_edges, bf16[32,128,256]{2,1,0:T(8,128)(2,1)} %copy-done.2, bf16[32,128,256]{2,1,0:T(8,128)(2,1)} %get-tuple-element.29.d_gate, f32[32,256]{1,0:T(8,128)S(1)} %get-tuple-element.30.mask, ...), custom_call_target="tpu_custom_call" | custom-call | flops 3489660928 | bytes 16777216 | tf_op jit(solution)/shard_map/back/pallas_call | solution.py:66
  230.4 19.2 %all_to_all.32.arrived = f32[128,8,128]{2,1,0:T(8,128)S(1)} all-to-all(f32[128,8,128]{2,1,0:T(8,128)S(1)} %bitcast.16), channel_id=1, replica_groups=mesh['grp'=4,'row'=32] {'grp','row'}, dimensions={0} | all-to-all | bytes 1048576 | tf_op jit(solution)/shard_map/all_to_all | solution.py:297
  249.5 0.2 total.1
  249.7 17.6 %all_to_all.33 = f32[128,8,128]{2,1,0:T(8,128)S(1)} all-to-all(f32[128,8,128]{2,1,0:T(8,128)S(1)} %total.1), channel_id=1, replica_groups=mesh['grp'=4,'row'=32] {'grp','row'}, dimensions={0} | all-to-all | bytes 1048576 | tf_op jit(solution)/shard_map/all_to_all | solution.py:297
  267.3 0.8 unpack.1
Async XLA Ops:
  7.4 62.8 %copy-start.2 = (bf16[32,128,256]{2,1,0:T(8,128)(2,1)}, bf16[32,128,256]{2,1,0:T(8,128)(2,1)S(1)}, u32[]{:S(2)}) copy-start(bf16[32,128,256]{2,1,0:T(8,128)(2,1)S(1)} %get-tuple-element.25.pair_t) | copy-start | bytes 6291460
  70.2 4.5 %copy-start = (bf16[128,2,32,256]{3,2,1,0:T(8,128)(2,1)}, bf16[128,2,32,256]{3,2,1,0:T(8,128)(2,1)S(1)}, u32[]{:S(2)}) copy-start(bf16[128,2,32,256]{3,2,1,0:T(8,128)(2,1)S(1)} %all_to_all.30) | copy-start | bytes 12582916
  74.7 34.9 %all-to-all-start.1 = ((bf16[128,32,256]{2,1,0:T(8,128)(2,1)}), bf16[128,32,256]{2,1,0:T(8,128)(2,1)S(1)}, u32[]{:S(2)}, u32[]{:S(2)}) async-start(bf16[128,32,256]{2,1,0:T(8,128)(2,1)} %bitcast.4), calls=%async_computation.1 | async-start | bytes 4194304 | tf_op jit(solution)/shard_map/all_to_all | solution.py:297
  116.2 34.3 %copy-start.1 = (bf16[128,2,32,256]{3,2,1,0:T(8,128)(2,1)S(1)}, bf16[128,2,32,256]{3,2,1,0:T(8,128)(2,1)}, u32[]{:S(2)}) copy-start(bf16[128,2,32,256]{3,2,1,0:T(8,128)(2,1)} %copy-done) | copy-start | bytes 12582916
  156.9 57.2 %all-to-all-start.3 = ((bf16[128,2,32,256]{3,2,1,0:T(8,128)(2,1)}), bf16[128,2,32,256]{3,2,1,0:T(8,128)(2,1)}, u32[]{:S(2)}, u32[]{:S(2)}) async-start(bf16[128,2,32,256]{3,2,1,0:T(8,128)(2,1)} %bitcast.17), calls=%async_computation.3 | async-start | bytes 8388608 | tf_op jit(solution)/shard_map/all_to_all | solution.py:297

commit v3 on v2

--- a/solution.py
+++ b/solution.py
@@ -10,7 +10,7 @@
 EPS = 1e-05
 AXES = ("grp", "row")
 RB = 16
-BATCH = 4
+BATCH = 1
 VMEM_LIMIT = 28 * 1024 * 1024
 F32 = jnp.float32
 BF16 = jnp.bfloat16
@@ -81,7 +81,7 @@
 
 
 def edges_kernel(
-    pair, row_tokens, col_tokens, gain, bias, w_in, edges, pair_t, mask, w_t, cols
+    pair, row_tokens, col_tokens, gain, bias, w_in, edges, mask, w_t, cols
 ):
     width = pair.shape[1]
     hidden = edges.shape[0]
@@ -99,9 +99,7 @@
 
     sides = [[], []]
     for r in range(RB):
-        x_t = pair[r].T
-        pair_t[r] = x_t
-        hat, _ = norm0(x_t.astype(F32))
+        hat, _ = norm0(pair[r].T.astype(F32))
         normed = (hat * cols[0] + cols[1]).astype(BF16)
         proj = dot(w_t[...], normed)
         m = col_mask * row_tokens[first_row + r].astype(F32)
@@ -114,7 +112,7 @@
         edges[:, side] = swap_rows(jnp.stack(sides[side]))
 
 
-def cotangent_kernel(pair_t, d_update, gain, bias, w_gate, d_proj, wg_t, cols):
+def cotangent_kernel(pair, d_update, gain, bias, w_gate, d_proj, pair_t, wg_t, cols):
     width = pair_t.shape[2]
 
     @pl.when(pl.program_id(0) == 0)
@@ -124,7 +122,9 @@
         cols[1] = columns(bias[...], width)
 
     for r in range(RB):
-        hat, _ = norm0(pair_t[r].astype(F32))
+        x_t = pair[r].T
+        pair_t[r] = x_t
+        hat, _ = norm0(x_t.astype(F32))
         normed = (hat * cols[0] + cols[1]).astype(BF16)
         gate = sigmoid(dot(wg_t[...], normed))
         d_proj[r] = (d_update[r].T.astype(F32) * gate).astype(BF16)
@@ -138,7 +138,7 @@
         out[h] = dot(left_t, right[h].reshape(depth, width)).astype(BF16)
 
 
-def d_tri_kernel(tri, d_proj, gain, w_out, d_tri, tri_t, cols):
+def d_tri_kernel(tri, d_proj, gain, w_out, d_tri, cols):
     width = tri.shape[2]
 
     @pl.when(pl.program_id(0) == 0)
@@ -146,7 +146,6 @@
         cols[...] = columns(gain[...], width)
 
     arrived = swap_rows(tri[...])
-    tri_t[...] = arrived
     grads = []
     for r in range(RB):
         hat, inv = norm0(arrived[r].astype(F32))
@@ -156,11 +155,12 @@
 
 
 def update_kernel(
-    tri_t, pair_t, d_update, gain, bias, w_gate, o_gain, o_bias, w_out,
+    tri, pair_t, d_update, gain, bias, w_gate, o_gain, o_bias, w_out,
     update, d_gate, sum_gate, sum_out, sum_norm,
-    wg_t, wo_t, cols, acc,
+    wg_t, wo_t, cols, acc, tri_t,
 ):
-    hidden, width = tri_t.shape[1:]
+    hidden, _, width = tri.shape
+    tri_t[...] = swap_rows(tri[...])
 
     @pl.when(pl.program_id(0) == 0)
     def _():
@@ -220,17 +220,40 @@
         out[g, :, 1] = right.astype(BF16).reshape(rows, tile_rows, width)
 
 
+def factors_kernel(pair_t, mask, gain, bias, w_in, factors, w_t, cols):
+    hidden = w_t.shape[0] // 4
+    width = pair_t.shape[2]
+
+    @pl.when(pl.program_id(0) == 0)
+    def _():
+        w_t[...] = w_in[...].T
+        cols[0] = columns(gain[...], width)
+        cols[1] = columns(bias[...], width)
+
+    for r in range(RB):
+        hat, _ = norm0(pair_t[r].astype(F32))
+        normed = (hat * cols[0] + cols[1]).astype(BF16)
+        proj = dot(w_t[...], normed)
+        m = mask[r : r + 1, :]
+        for side in range(2):
+            first = side * 2 * hidden
+            gate = sigmoid(proj[first : first + hidden])
+            value = proj[first + hidden : first + 2 * hidden]
+            gate_m = gate * m
+            factors[r, first : first + hidden] = (gate_m * value * (1.0 - gate)).astype(BF16)
+            factors[r, first + hidden : first + 2 * hidden] = gate_m.astype(BF16)
+
+
 def back_kernel(
-    d_edges, pair_t, d_gate, mask, gain, bias, w_in, w_gate, sum_gate, sum_out, sum_norm,
+    d_edges, pair_t, d_gate, factors, gain, bias, w_in, w_gate, sum_gate, sum_out, sum_norm,
     d_pair, sums,
-    w_t, w_all, cols, acc, acc_in,
+    w_all, cols, acc, acc_in, rows_f,
 ):
     hidden = d_edges.shape[0]
     chans, width = pair_t.shape[1:]
 
     @pl.when(pl.program_id(0) == 0)
     def _():
-        w_t[...] = w_in[...].T
         w_all[:, : 4 * hidden] = w_in[...]
         w_all[:, 4 * hidden :] = w_gate[...]
         cols[0] = columns(gain[...], width)
@@ -244,16 +267,13 @@
         for r in range(first_row, first_row + BATCH):
             hat, inv = norm0(pair_t[r].astype(F32))
             normed = (hat * cols[0] + cols[1]).astype(BF16)
-            proj = dot(w_t[...], normed)
-            m = mask[r : r + 1, :]
-            parts = []
-            for side in range(2):
-                gate = sigmoid(proj[side * 2 * hidden : (side * 2 + 1) * hidden])
-                value = proj[(side * 2 + 1) * hidden : (side * 2 + 2) * hidden]
-                d_value = arrived[side][r].astype(F32) * m * gate
-                parts.append((d_value * value * (1.0 - gate)).astype(BF16))
-                parts.append(d_value.astype(BF16))
-            d_projected = jnp.concatenate(parts, axis=0)
+            d_projected = jnp.concatenate(
+                [
+                    arrived[part // 2][r] * factors[r, part * hidden : (part + 1) * hidden]
+                    for part in range(4)
+                ],
+                axis=0,
+            )
             left.append(normed)
             right.append(d_projected)
             d_normed = dot(w_all[...], jnp.concatenate([d_projected, d_gate[r]], axis=0))
@@ -269,26 +289,32 @@
         second = jnp.sum(acc[1], axis=1, keepdims=True)
         norms = jnp.where(lane == 0, first, jnp.where(lane == 1, second, sum_norm[...]))
         for q in range(4):
-            sums[pl.ds(q, chans, stride=8), :] = acc_in[:, q * 128 : (q + 1) * 128]
-        sums[pl.ds(4, chans, stride=8), :] = sum_gate[...]
-        sums[pl.ds(5, chans, stride=8), :] = sum_out[...]
-        sums[pl.ds(6, chans, stride=8), :] = norms
-        sums[pl.ds(7, chans, stride=8), :] = norms
+            rows_f[pl.ds(q, chans, stride=8), :] = acc_in[:, q * 128 : (q + 1) * 128]
+        rows_f[pl.ds(4, chans, stride=8), :] = sum_gate[...]
+        rows_f[pl.ds(5, chans, stride=8), :] = sum_out[...]
+        rounded = norms.astype(BF16).astype(F32)
+        rows_f[pl.ds(6, chans, stride=8), :] = rounded
+        rows_f[pl.ds(7, chans, stride=8), :] = norms - rounded
+        sums[...] = rows_f[...].reshape(sums.shape).astype(BF16)
 
 
 def total_kernel(scale, arrived, out):
-    out[...] = jnp.broadcast_to(
-        jnp.sum(arrived[...], axis=0, keepdims=True) * scale, out.shape
-    )
-
-
-def unpack_kernel(sums, d_w_in, d_w_gate, d_w_out, d_in_norm, d_out_norm):
+    total = jnp.sum(arrived[...].astype(F32), axis=0) * scale
+    row = lax.broadcasted_iota(jnp.int32, total.shape, 0)
+    norms = total[6:7] + total[7:8]
+    rounded = norms.astype(BF16).astype(F32)
+    total = jnp.where(row == 6, rounded, jnp.where(row == 7, norms - rounded, total))
+    out[...] = jnp.broadcast_to(total.astype(BF16)[None], out.shape)
+
+
+def unpack_kernel(sums, d_w_in, d_w_gate, d_w_out, d_in_norm, d_out_norm, rows_f):
     chans = d_w_in.shape[0]
+    rows_f[...] = sums[...].astype(F32).reshape(rows_f.shape)
     for q in range(4):
-        d_w_in[:, q * 128 : (q + 1) * 128] = sums[pl.ds(q, chans, stride=8), :]
-    d_w_gate[...] = sums[pl.ds(4, chans, stride=8), :]
-    d_w_out[...] = sums[pl.ds(5, chans, stride=8), :]
-    norms = sums[pl.ds(6, chans, stride=8), :].T
+        d_w_in[:, q * 128 : (q + 1) * 128] = rows_f[pl.ds(q, chans, stride=8), :]
+    d_w_gate[...] = rows_f[pl.ds(4, chans, stride=8), :]
+    d_w_out[...] = rows_f[pl.ds(5, chans, stride=8), :]
+    norms = (rows_f[pl.ds(6, chans, stride=8), :] + rows_f[pl.ds(7, chans, stride=8), :]).T
     d_in_norm[...] = norms[0:2]
     d_out_norm[...] = norms[2:4]
 
@@ -319,9 +345,10 @@
     maskblock = pl.BlockSpec((RB, tile_cols), lambda s: (s, 0))
     edgeblock = pl.BlockSpec((hidden, 2, RB, tile_cols), lambda s: (0, 0, s, 0))
     triblock = pl.BlockSpec((hidden, RB, tile_cols), lambda s: (0, s, 0))
+    factorblock = pl.BlockSpec((RB, 4 * hidden, tile_cols), lambda s: (s, 0, 0))
     t_shape = sds((tile_rows, chans, tile_cols), BF16)
 
-    edges, pair_t, mask_pair = call(
+    edges, mask_pair = call(
         edges_kernel, "edges", (steps,),
         [
             rowblock, pl.BlockSpec(memory_space=pltpu.SMEM), whole((tokens // 128, 128)),
@@ -329,8 +356,7 @@
         ],
         [
             (edgeblock, sds((hidden, 2, tile_rows, tile_cols), BF16)),
-            (chanblock, t_shape),
-            (maskblock, sds((tile_rows, tile_cols), F32)),
+            (maskblock, pltpu.HBM((tile_rows, tile_cols), F32)),
         ],
         [
             pltpu.VMEM((4 * hidden, chans), BF16),
@@ -341,13 +367,13 @@
         in_hbm=(0, 2, 3, 4, 5),
     )
     chan_edges = exchange(edges)
-    (d_proj,) = call(
+    d_proj, pair_t = call(
         cotangent_kernel, "cotangent", (steps,),
-        [chanblock, rowblock, vec, vec, square],
-        [(chanblock, pltpu.HBM(t_shape.shape, BF16))],
+        [rowblock, rowblock, vec, vec, square],
+        [(chanblock, pltpu.HBM(t_shape.shape, BF16))] * 2,
         [pltpu.VMEM((chans, hidden), BF16), pltpu.VMEM((2, chans, tile_cols), F32)],
         2 * positions * chans * hidden, 8 * positions * chans,
-        (pair_t, d_update, gain, bias, w_gate),
+        (pair, d_update, gain, bias, w_gate),
     )
     chan_edges = chan_edges.reshape(groups, rows, 2, tile_rows, tile_cols)
     (triangle,) = call(
@@ -359,7 +385,7 @@
         [
             (
                 pl.BlockSpec((groups, tile_cols, tile_cols), lambda g: (0, g, 0)),
-                sds((groups, tokens, tile_cols), BF16),
+                pltpu.HBM((groups, tokens, tile_cols), BF16),
             )
         ],
         [],
@@ -368,12 +394,11 @@
         in_hbm=(),
     )
     tri = exchange(triangle.reshape(devices, tile_rows, tile_cols))
-    d_tri, tri_t = call(
+    (d_tri,) = call(
         d_tri_kernel, "d_tri", (steps,),
         [triblock, chanblock, vec, square],
         [
             (triblock, sds((hidden, tile_rows, tile_cols), BF16)),
-            (chanblock, pltpu.HBM(t_shape.shape, BF16)),
         ],
         [
             pltpu.VMEM((hidden, tile_cols), F32),
@@ -385,7 +410,7 @@
     chan_d_tri = exchange(d_tri)
     update, d_gate, sum_gate, sum_out, sum_norm = call(
         update_kernel, "update", (steps,),
-        [chanblock, chanblock, rowblock, vec, vec, square, vec, vec, square],
+        [triblock, chanblock, rowblock, vec, vec, square, vec, vec, square],
         [
             (rowblock, sds((tile_rows, tile_cols, chans), BF16)),
             (chanblock, pltpu.HBM(t_shape.shape, BF16)),
@@ -398,9 +423,10 @@
             pltpu.VMEM((chans, hidden), BF16),
             pltpu.VMEM((4, chans, tile_cols), F32),
             pltpu.VMEM((2, hidden, 128), F32),
+            pltpu.VMEM((RB, hidden, tile_cols), BF16),
         ],
         10 * positions * chans * hidden, 16 * positions * chans,
-        (tri_t, pair_t, d_update, gain, bias, w_gate, o_gain, o_bias, w_out),
+        (tri, pair_t, d_update, gain, bias, w_gate, o_gain, o_bias, w_out),
     )
     depth_rows = rows // groups
     edge_rows = pl.BlockSpec(
@@ -416,42 +442,50 @@
         in_hbm=(),
     )
     d_edges = exchange(d_chan_edges.reshape(devices, 2, tile_rows, tile_cols))
+    (factors,) = call(
+        factors_kernel, "factors", (steps,),
+        [chanblock, maskblock, vec, vec, wide],
+        [(factorblock, pltpu.HBM((tile_rows, 4 * hidden, tile_cols), BF16))],
+        [pltpu.VMEM((4 * hidden, chans), BF16), pltpu.VMEM((2, chans, tile_cols), F32)],
+        2 * positions * chans * 4 * hidden, 10 * positions * chans,
+        (pair_t, mask_pair, gain, bias, w_in),
+    )
     d_pair, sums = call(
         back_kernel, "back", (steps,),
-        [edgeblock, chanblock, chanblock, maskblock, vec, vec, wide, square, square, square,
+        [edgeblock, chanblock, chanblock, factorblock, vec, vec, wide, square, square, square,
          whole((hidden, 128))],
         [
             (rowblock, sds((tile_rows, tile_cols, chans), BF16)),
-            (whole((chans * 8, 128)), sds((chans * 8, 128), F32)),
-        ],
-        [
-            pltpu.VMEM((4 * hidden, chans), BF16),
+            (whole((chans, 8, 128)), sds((chans, 8, 128), BF16)),
+        ],
+        [
             pltpu.VMEM((chans, 4 * hidden + chans), BF16),
             pltpu.VMEM((2, chans, tile_cols), F32),
             pltpu.VMEM((2, chans, 128), F32),
             pltpu.VMEM((chans, 4 * hidden), F32),
+            pltpu.VMEM((chans * 8, 128), F32),
         ],
         26 * positions * chans * hidden, 16 * positions * chans,
-        (d_edges, pair_t, d_gate, mask_pair, gain, bias, w_in, w_gate, sum_gate, sum_out, sum_norm),
-        in_hbm=(0, 1, 2, 4, 5, 6, 7),
-    )
-    part = sds((devices, 8, 128), F32)
-    arrived = exchange(sums.reshape(devices, 8, 128))
+        (d_edges, pair_t, d_gate, factors, gain, bias, w_in, w_gate, sum_gate, sum_out, sum_norm),
+        in_hbm=(0, 1, 2, 3, 4, 5, 6, 7),
+    )
+    part = sds((devices, 8, 128), BF16)
+    arrived = exchange(sums)
     (total,) = call(
         functools.partial(total_kernel, 1.0 / tokens), "total", (1,),
         [whole(part.shape)], [(whole(part.shape), part)], [],
         devices * 1024, devices * 8192, (arrived,),
         in_hbm=(),
     )
-    everywhere = exchange(total).reshape(chans * 8, 128)
+    everywhere = exchange(total)
     small = [
         (chans, 4 * hidden), (chans, chans), (hidden, chans), (2, chans), (2, hidden),
     ]
     grads = call(
         unpack_kernel, "unpack", (1,),
-        [whole((chans * 8, 128))],
+        [whole((chans, 8, 128))],
         [(whole(shape), sds(shape, F32)) for shape in small],
-        [], 1024, devices * 8192, (everywhere,),
+        [pltpu.VMEM((chans * 8, 128), F32)], 1024, devices * 8192, (everywhere,),
         in_hbm=(),
     )
     return (update, d_pair, *grads)

time: 268 us -> 258 us (0.963)
  waiting for transfers between devices: 61.7 us -> 53.4 us
  blocking collectives: 134 us -> 128 us
  Pallas kernels: 60.5 us -> 63.8 us
    all_to_all x2, waiting for transfers between devices: 61.7 us -> 53.4 us  [exchange(): return lax.all_to_all(chunks, AXES, split_axis=0, concat_axis=0, tiled=True)]
    all_to_all x4, blocking collectives: 134 us -> 128 us  [exchange(): return lax.all_to_all(chunks, AXES, split_axis=0, concat_axis=0, tiled=True)]
    pallas_call x9 -> x10, Pallas kernels: 60.5 us -> 63.8 us  [call(): pl.pallas_call(kernel, name=name, grid=grid, in_specs=ins, out_specs=[spe...]
  transfers between devices with their start and end apart: 2 -> 2, of which waited for: 2 -> 2; matrix products, arithmetic and copies ran while one was open for 0% -> 0% of each run, Pallas kernels for 7% -> 11%
where the time goes in v3:
time: 258 us
  blocking collectives  128 us (50%)
  Pallas kernels  63.8 us (25%)
  waiting for transfers between devices  53.4 us (21%)
  starting transfers between devices  11.5 us (4%)
    all_to_all x4, blocking collectives, exchange(): return lax.all_to_all(chunks, AXES, split_axis=0, concat_axis=0, tiled=True)  128 us
    pallas_call x10, Pallas kernels, call(): pl.pallas_call(kernel, name=name, grid=grid, in_specs=ins, out_specs=[spe...  63.8 us
    all_to_all x2, waiting for transfers between devices, exchange(): return lax.all_to_all(chunks, AXES, split_axis=0, concat_axis=0, tiled=True)  53.4 us
    all_to_all x2, starting transfers between devices, exchange(): return lax.all_to_all(chunks, AXES, split_axis=0, concat_axis=0, tiled=True)  11.5 us
  transfers between devices with their start and end apart: 2, of which 2 were waited for; matrix products, arithmetic and copies ran while one was open for 0% of the time, Pallas kernels for 11%

profile of v3, /device:TPU:1, one launch (start us, length us, event | category | flops | bytes accessed | tf_op | source)
XLA Modules:
  0.0 257.8 jit_solution(4051821116320388414)
XLA Ops:
  0.6 7.3 %edges.1 = (bf16[128,2,32,256]{3,2,1,0:T(8,128)(2,1)S(1)}, f32[32,256]{1,0:T(8,128)}) custom-call(bf16[32,256,128]{2,1,0:T(8,128)(2,1)} %pair.3, s32[1024]{0:T(1024)} %row_tokens.1, s32[8,128]{1,0:T(8,128)} %bitcast.28, f32[1,128]{1,0:T(1,128)} %bitcast.15, f32[1,128]{1,0:T(1,128)} %bitcast.20, bf16[128,512]{1,0:T(8,128)(2,1)} %w_in.5), custom_call_target="tpu_custom_call" | custom-call | flops 1073741824 | bytes 16777216 | tf_op jit(solution)/shard_map/edges/pallas_call | solution.py:66
  7.9 62.7 %all_to_all.30 = bf16[128,2,32,256]{3,2,1,0:T(8,128)(2,1)S(1)} all-to-all(bf16[128,2,32,256]{3,2,1,0:T(8,128)(2,1)S(1)} %get-tuple-element.23), channel_id=1, replica_groups=mesh['grp'=4,'row'=32] {'grp','row'}, dimensions={0} | all-to-all | bytes 8388608 | tf_op jit(solution)/shard_map/all_to_all | solution.py:323
  70.7 0.0 copy-start
  70.7 4.5 %triangle.1 = bf16[4,1024,256]{2,1,0:T(8,128)(2,1)} custom-call(bf16[4,32,2,32,256]{4,3,2,1,0:T(8,128)(2,1)S(1)} %bitcast.9, bf16[4,32,2,32,256]{4,3,2,1,0:T(8,128)(2,1)S(1)} %bitcast.10), custom_call_target="tpu_custom_call" | custom-call | flops 2147483648 | bytes 6291456 | tf_op jit(solution)/shard_map/triangle/pallas_call | solution.py:66
  75.2 0.0 copy-done
  75.2 5.5 %all-to-all-start.1 = ((bf16[128,32,256]{2,1,0:T(8,128)(2,1)}), bf16[128,32,256]{2,1,0:T(8,128)(2,1)S(1)}, u32[]{:S(2)}, u32[]{:S(2)}) async-start(bf16[128,32,256]{2,1,0:T(8,128)(2,1)} %bitcast.13), calls=%async_computation.1 | async-start | bytes 4194304 | tf_op jit(solution)/shard_map/all_to_all | solution.py:323
  80.6 5.3 %cotangent.1 = (bf16[32,128,256]{2,1,0:T(8,128)(2,1)}, bf16[32,128,256]{2,1,0:T(8,128)(2,1)}) custom-call(bf16[32,256,128]{2,1,0:T(8,128)(2,1)} %pair.3, bf16[32,256,128]{2,1,0:T(8,128)(2,1)} %d_update.3, f32[1,128]{1,0:T(1,128)} %bitcast.16, f32[1,128]{1,0:T(1,128)} %bitcast.21, bf16[128,128]{1,0:T(8,128)(2,1)} %w_gate.5), custom_call_target="tpu_custom_call" | custom-call | flops 268435456 | bytes 8388608 | tf_op jit(solution)/shard_map/cotangent/pallas_call | solution.py:66
  86.0 24.1 %all-to-all-done.1.tri = bf16[128,32,256]{2,1,0:T(8,128)(2,1)S(1)} async-done(((bf16[128,32,256]{2,1,0:T(8,128)(2,1)}), bf16[128,32,256]{2,1,0:T(8,128)(2,1)S(1)}, u32[]{:S(2)}, u32[]{:S(2)}) %all-to-all-start.1) | async-done | bytes 2097184 | tf_op jit(solution)/shard_map/all_to_all | solution.py:323
  110.0 0.0 copy-start.2
  110.0 6.4 %d_tri.1 = bf16[128,32,256]{2,1,0:T(8,128)(2,1)S(1)} custom-call(bf16[128,32,256]{2,1,0:T(8,128)(2,1)S(1)} %all-to-all-done.1.tri, bf16[32,128,256]{2,1,0:T(8,128)(2,1)} %get-tuple-element.26.d_proj, f32[1,128]{1,0:T(1,128)} %bitcast.25, bf16[128,128]{1,0:T(8,128)(2,1)} %w_out.3), custom_call_target="tpu_custom_call" | custom-call | flops 268435456 | bytes 8388608 | tf_op jit(solution)/shard_map/d_tri/pallas_call | solution.py:66
  116.5 0.0 copy-done.2
  116.5 0.0 copy-start.1
  116.5 34.3 %all_to_all.31 = bf16[128,32,256]{2,1,0:T(8,128)(2,1)S(1)} all-to-all(bf16[128,32,256]{2,1,0:T(8,128)(2,1)S(1)} %d_tri.1), channel_id=1, replica_groups=mesh['grp'=4,'row'=32] {'grp','row'}, dimensions={0} | all-to-all | bytes 4194304 | tf_op jit(solution)/shard_map/all_to_all | solution.py:323
  150.8 0.0 copy-done.1
  150.8 6.4 %d_edges.1 = bf16[4,32,2,32,256]{4,3,2,1,0:T(8,128)(2,1)} custom-call(bf16[4,32,2,32,256]{4,3,2,1,0:T(8,128)(2,1)S(1)} %bitcast.11, bf16[4,1024,256]{2,1,0:T(8,128)(2,1)S(1)} %bitcast.12), custom_call_target="tpu_custom_call" | custom-call | flops 4294967296 | bytes 10485760 | tf_op jit(solution)/shard_map/d_edges/pallas_call | solution.py:66
  157.1 6.0 %all-to-all-start.3 = ((bf16[128,2,32,256]{3,2,1,0:T(8,128)(2,1)}), bf16[128,2,32,256]{3,2,1,0:T(8,128)(2,1)}, u32[]{:S(2)}, u32[]{:S(2)}) async-start(bf16[128,2,32,256]{3,2,1,0:T(8,128)(2,1)} %bitcast.14), calls=%async_computation.3 | async-start | bytes 8388608 | tf_op jit(solution)/shard_map/all_to_all | solution.py:323
  163.1 8.0 %factors.1 = bf16[32,512,256]{2,1,0:T(8,128)(2,1)} custom-call(bf16[32,128,256]{2,1,0:T(8,128)(2,1)} %get-tuple-element.24.pair_t, f32[32,256]{1,0:T(8,128)} %get-tuple-element.28.mask, f32[1,128]{1,0:T(1,128)} %bitcast.17, f32[1,128]{1,0:T(1,128)} %bitcast.22, bf16[128,512]{1,0:T(8,128)(2,1)} %w_in.5), custom_call_target="tpu_custom_call" | custom-call | flops 1073741824 | bytes 10485760 | tf_op jit(solution)/shard_map/factors/pallas_call | solution.py:66
  171.1 13.9 %update.1 = (bf16[32,256,128]{2,1,0:T(8,128)(2,1)}, bf16[32,128,256]{2,1,0:T(8,128)(2,1)}, f32[128,128]{1,0:T(8,128)S(1)}, f32[128,128]{1,0:T(8,128)S(1)}, f32[128,128]{1,0:T(8,128)S(1)}) custom-call(bf16[128,32,256]{2,1,0:T(8,128)(2,1)} %copy-done.2, bf16[32,128,256]{2,1,0:T(8,128)(2,1)} %get-tuple-element.24.pair_t, bf16[32,256,128]{2,1,0:T(8,128)(2,1)} %d_update.3, ...), custom_call_target="tpu_custom_call" | custom-call | flops 1342177280 | bytes 16777216 | tf_op jit(solution)/shard_map/update/pallas_call | solution.py:66
  185.0 29.4 %all-to-all-done.3.d_edges = bf16[128,2,32,256]{3,2,1,0:T(8,128)(2,1)} async-done(((bf16[128,2,32,256]{3,2,1,0:T(8,128)(2,1)}), bf16[128,2,32,256]{3,2,1,0:T(8,128)(2,1)}, u32[]{:S(2)}, u32[]{:S(2)}) %all-to-all-start.3) | async-done | bytes 4194336 | tf_op jit(solution)/shard_map/all_to_all | solution.py:323
  214.3 11.1 %back.1 = (bf16[32,256,128]{2,1,0:T(8,128)(2,1)}, bf16[128,8,128]{2,1,0:T(8,128)(2,1)S(1)}) custom-call(bf16[128,2,32,256]{3,2,1,0:T(8,128)(2,1)} %all-to-all-done.3.d_edges, bf16[32,128,256]{2,1,0:T(8,128)(2,1)} %get-tuple-element.24.pair_t, bf16[32,128,256]{2,1,0:T(8,128)(2,1)} %get-tuple-element.27.d_gate, bf16[32,512,256]{2,1,0:T(8,128)(2,1)} %factors.1, ...), custom_call_target="tpu_custom_call" | custom-call | flops 3489660928 | bytes 16777216 | tf_op jit(solution)/shard_map/back/pallas_call | solution.py:66
  225.4 16.5 %all_to_all.32.arrived = bf16[128,8,128]{2,1,0:T(8,128)(2,1)S(1)} all-to-all(bf16[128,8,128]{2,1,0:T(8,128)(2,1)S(1)} %get-tuple-element.33), channel_id=1, replica_groups=mesh['grp'=4,'row'=32] {'grp','row'}, dimensions={0} | all-to-all | bytes 524288 | tf_op jit(solution)/shard_map/all_to_all | solution.py:323
  241.9 0.2 total.1
  242.1 14.9 %all_to_all.33.sums = bf16[128,8,128]{2,1,0:T(8,128)(2,1)S(1)} all-to-all(bf16[128,8,128]{2,1,0:T(8,128)(2,1)S(1)} %total.1), channel_id=1, replica_groups=mesh['grp'=4,'row'=32] {'grp','row'}, dimensions={0} | all-to-all | bytes 524288 | tf_op jit(solution)/shard_map/all_to_all | solution.py:323
  256.9 0.9 unpack.1
Async XLA Ops:
  70.7 4.5 %copy-start = (bf16[128,2,32,256]{3,2,1,0:T(8,128)(2,1)}, bf16[128,2,32,256]{3,2,1,0:T(8,128)(2,1)S(1)}, u32[]{:S(2)}) copy-start(bf16[128,2,32,256]{3,2,1,0:T(8,128)(2,1)S(1)} %all_to_all.30) | copy-start | bytes 12582916
  75.2 34.8 %all-to-all-start.1 = ((bf16[128,32,256]{2,1,0:T(8,128)(2,1)}), bf16[128,32,256]{2,1,0:T(8,128)(2,1)S(1)}, u32[]{:S(2)}, u32[]{:S(2)}) async-start(bf16[128,32,256]{2,1,0:T(8,128)(2,1)} %bitcast.13), calls=%async_computation.1 | async-start | bytes 4194304 | tf_op jit(solution)/shard_map/all_to_all | solution.py:323
  110.0 6.5 %copy-start.2 = (bf16[128,32,256]{2,1,0:T(8,128)(2,1)}, bf16[128,32,256]{2,1,0:T(8,128)(2,1)S(1)}, u32[]{:S(2)}) copy-start(bf16[128,32,256]{2,1,0:T(8,128)(2,1)S(1)} %all-to-all-done.1.tri) | copy-start | bytes 6291460
  116.5 34.3 %copy-start.1 = (bf16[128,2,32,256]{3,2,1,0:T(8,128)(2,1)S(1)}, bf16[128,2,32,256]{3,2,1,0:T(8,128)(2,1)}, u32[]{:S(2)}) copy-start(bf16[128,2,32,256]{3,2,1,0:T(8,128)(2,1)} %copy-done) | copy-start | bytes 12582916
  157.1 57.2 %all-to-all-start.3 = ((bf16[128,2,32,256]{3,2,1,0:T(8,128)(2,1)}), bf16[128,2,32,256]{3,2,1,0:T(8,128)(2,1)}, u32[]{:S(2)}, u32[]{:S(2)}) async-start(bf16[128,2,32,256]{3,2,1,0:T(8,128)(2,1)} %bitcast.14), calls=%async_computation.3 | async-start | bytes 8388608 | tf_op jit(solution)/shard_map/all_to_all | solution.py:323

commit v4 on v3

--- a/solution.py
+++ b/solution.py
@@ -80,16 +80,21 @@
     return pl.BlockSpec(shape, lambda *_: (0,) * len(shape))
 
 
-def edges_kernel(
-    pair, row_tokens, col_tokens, gain, bias, w_in, edges, mask, w_t, cols
-):
-    width = pair.shape[1]
-    hidden = edges.shape[0]
+def masks(row_tokens, col_tokens, width):
     first_row = (lax.axis_index("row") * pl.num_programs(0) + pl.program_id(0)) * RB
     first_col = lax.axis_index("grp") * (width // 128)
     col_mask = jnp.concatenate(
         [col_tokens[pl.ds(first_col + i, 1), :] for i in range(width // 128)], axis=1
     ).astype(F32)
+    return lambda r: col_mask * row_tokens[first_row + r].astype(F32)
+
+
+def edges_kernel(
+    pair, row_tokens, col_tokens, gain, bias, w_in, edges, w_t, cols
+):
+    width = pair.shape[1]
+    hidden = edges.shape[0]
+    row_mask = masks(row_tokens, col_tokens, width)
 
     @pl.when(pl.program_id(0) == 0)
     def _():
@@ -102,8 +107,7 @@
         hat, _ = norm0(pair[r].T.astype(F32))
         normed = (hat * cols[0] + cols[1]).astype(BF16)
         proj = dot(w_t[...], normed)
-        m = col_mask * row_tokens[first_row + r].astype(F32)
-        mask[r : r + 1, :] = m
+        m = row_mask(r)
         for side in range(2):
             gate = sigmoid(proj[side * 2 * hidden : (side * 2 + 1) * hidden])
             value = proj[(side * 2 + 1) * hidden : (side * 2 + 2) * hidden]
@@ -220,9 +224,10 @@
         out[g, :, 1] = right.astype(BF16).reshape(rows, tile_rows, width)
 
 
-def factors_kernel(pair_t, mask, gain, bias, w_in, factors, w_t, cols):
+def factors_kernel(pair_t, row_tokens, col_tokens, gain, bias, w_in, factors, w_t, cols):
     hidden = w_t.shape[0] // 4
     width = pair_t.shape[2]
+    row_mask = masks(row_tokens, col_tokens, width)
 
     @pl.when(pl.program_id(0) == 0)
     def _():
@@ -234,7 +239,7 @@
         hat, _ = norm0(pair_t[r].astype(F32))
         normed = (hat * cols[0] + cols[1]).astype(BF16)
         proj = dot(w_t[...], normed)
-        m = mask[r : r + 1, :]
+        m = row_mask(r)
         for side in range(2):
             first = side * 2 * hidden
             gate = sigmoid(proj[first : first + hidden])
@@ -342,28 +347,27 @@
     wide = whole((chans, 4 * hidden))
     rowblock = pl.BlockSpec((RB, tile_cols, chans), lambda s: (s, 0, 0))
     chanblock = pl.BlockSpec((RB, chans, tile_cols), lambda s: (s, 0, 0))
-    maskblock = pl.BlockSpec((RB, tile_cols), lambda s: (s, 0))
+    token_lanes = token_mask.reshape(tokens // 128, 128)
+    token_specs = [pl.BlockSpec(memory_space=pltpu.SMEM), whole(token_lanes.shape)]
     edgeblock = pl.BlockSpec((hidden, 2, RB, tile_cols), lambda s: (0, 0, s, 0))
     triblock = pl.BlockSpec((hidden, RB, tile_cols), lambda s: (0, s, 0))
     factorblock = pl.BlockSpec((RB, 4 * hidden, tile_cols), lambda s: (s, 0, 0))
     t_shape = sds((tile_rows, chans, tile_cols), BF16)
 
-    edges, mask_pair = call(
+    (edges,) = call(
         edges_kernel, "edges", (steps,),
         [
-            rowblock, pl.BlockSpec(memory_space=pltpu.SMEM), whole((tokens // 128, 128)),
-            vec, vec, wide,
+            rowblock, *token_specs, vec, vec, wide,
         ],
         [
             (edgeblock, sds((hidden, 2, tile_rows, tile_cols), BF16)),
-            (maskblock, pltpu.HBM((tile_rows, tile_cols), F32)),
         ],
         [
             pltpu.VMEM((4 * hidden, chans), BF16),
             pltpu.VMEM((2, chans, tile_cols), F32),
         ],
         2 * positions * chans * 4 * hidden, 16 * positions * chans,
-        (pair, token_mask, token_mask.reshape(tokens // 128, 128), gain, bias, w_in),
+        (pair, token_mask, token_lanes, gain, bias, w_in),
         in_hbm=(0, 2, 3, 4, 5),
     )
     chan_edges = exchange(edges)
@@ -444,11 +448,12 @@
     d_edges = exchange(d_chan_edges.reshape(devices, 2, tile_rows, tile_cols))
     (factors,) = call(
         factors_kernel, "factors", (steps,),
-        [chanblock, maskblock, vec, vec, wide],
+        [chanblock, *token_specs, vec, vec, wide],
         [(factorblock, pltpu.HBM((tile_rows, 4 * hidden, tile_cols), BF16))],
         [pltpu.VMEM((4 * hidden, chans), BF16), pltpu.VMEM((2, chans, tile_cols), F32)],
         2 * positions * chans * 4 * hidden, 10 * positions * chans,
-        (pair_t, mask_pair, gain, bias, w_in),
+        (pair_t, token_mask, token_lanes, gain, bias, w_in),
+        in_hbm=(0, 2, 3, 4, 5),
     )
     d_pair, sums = call(
         back_kernel, "back", (steps,),
@@ -467,7 +472,7 @@
         ],
         26 * positions * chans * hidden, 16 * positions * chans,
         (d_edges, pair_t, d_gate, factors, gain, bias, w_in, w_gate, sum_gate, sum_out, sum_norm),
-        in_hbm=(0, 1, 2, 3, 4, 5, 6, 7),
+        in_hbm=(1, 2, 3, 4, 5, 6, 7),
     )
     part = sds((devices, 8, 128), BF16)
     arrived = exchange(sums)

time: 258 us -> 258 us (level)
  no operation moved by 1% of the time
where the time goes in v4:
time: 258 us; the launch traced here: 257 us
  blocking collectives  128 us (50%)
  Pallas kernels  63.4 us (25%)
  waiting for transfers between devices  53.3 us (21%)
  starting transfers between devices  11.5 us (4%)
    all_to_all x4, blocking collectives, exchange(): return lax.all_to_all(chunks, AXES, split_axis=0, concat_axis=0, tiled=True)  128 us
    pallas_call x10, Pallas kernels, call(): pl.pallas_call(kernel, name=name, grid=grid, in_specs=ins, out_specs=[spe...  63.4 us
    all_to_all x2, waiting for transfers between devices, exchange(): return lax.all_to_all(chunks, AXES, split_axis=0, concat_axis=0, tiled=True)  53.3 us
    all_to_all x2, starting transfers between devices, exchange(): return lax.all_to_all(chunks, AXES, split_axis=0, concat_axis=0, tiled=True)  11.5 us
  transfers between devices with their start and end apart: 2, of which 2 were waited for; matrix products, arithmetic and copies ran while one was open for 0% of the time, Pallas kernels for 11%

profile of v4, /device:TPU:1, one launch (start us, length us, event | category | flops | bytes accessed | tf_op | source)
XLA Modules:
  0.0 257.3 jit_solution(2480968620161181795)
XLA Ops:
  0.6 6.7 %edges.1 = bf16[128,2,32,256]{3,2,1,0:T(8,128)(2,1)S(1)} custom-call(bf16[32,256,128]{2,1,0:T(8,128)(2,1)} %pair.3, s32[1024]{0:T(1024)} %row_tokens.3, s32[8,128]{1,0:T(8,128)} %bitcast.15, f32[1,128]{1,0:T(1,128)} %bitcast.17, f32[1,128]{1,0:T(1,128)} %bitcast.22, bf16[128,512]{1,0:T(8,128)(2,1)} %w_in.5), custom_call_target="tpu_custom_call" | custom-call | flops 1073741824 | bytes 16777216 | tf_op jit(solution)/shard_map/edges/pallas_call | solution.py:66
  7.3 62.7 %all_to_all.30 = bf16[128,2,32,256]{3,2,1,0:T(8,128)(2,1)S(1)} all-to-all(bf16[128,2,32,256]{3,2,1,0:T(8,128)(2,1)S(1)} %edges.1), channel_id=1, replica_groups=mesh['grp'=4,'row'=32] {'grp','row'}, dimensions={0} | all-to-all | bytes 8388608 | tf_op jit(solution)/shard_map/all_to_all | solution.py:328
  70.1 0.0 copy-start
  70.1 4.5 %triangle.1 = bf16[4,1024,256]{2,1,0:T(8,128)(2,1)} custom-call(bf16[4,32,2,32,256]{4,3,2,1,0:T(8,128)(2,1)S(1)} %bitcast.9, bf16[4,32,2,32,256]{4,3,2,1,0:T(8,128)(2,1)S(1)} %bitcast.10), custom_call_target="tpu_custom_call" | custom-call | flops 2147483648 | bytes 6291456 | tf_op jit(solution)/shard_map/triangle/pallas_call | solution.py:66
  74.6 0.0 copy-done
  74.6 5.5 %all-to-all-start.1 = ((bf16[128,32,256]{2,1,0:T(8,128)(2,1)}), bf16[128,32,256]{2,1,0:T(8,128)(2,1)S(1)}, u32[]{:S(2)}, u32[]{:S(2)}) async-start(bf16[128,32,256]{2,1,0:T(8,128)(2,1)} %bitcast.13), calls=%async_computation.1 | async-start | bytes 4194304 | tf_op jit(solution)/shard_map/all_to_all | solution.py:328
  80.1 5.3 %cotangent.1 = (bf16[32,128,256]{2,1,0:T(8,128)(2,1)}, bf16[32,128,256]{2,1,0:T(8,128)(2,1)}) custom-call(bf16[32,256,128]{2,1,0:T(8,128)(2,1)} %pair.3, bf16[32,256,128]{2,1,0:T(8,128)(2,1)} %d_update.3, f32[1,128]{1,0:T(1,128)} %bitcast.18, f32[1,128]{1,0:T(1,128)} %bitcast.23, bf16[128,128]{1,0:T(8,128)(2,1)} %w_gate.5), custom_call_target="tpu_custom_call" | custom-call | flops 268435456 | bytes 8388608 | tf_op jit(solution)/shard_map/cotangent/pallas_call | solution.py:66
  85.4 24.1 %all-to-all-done.1.tri = bf16[128,32,256]{2,1,0:T(8,128)(2,1)S(1)} async-done(((bf16[128,32,256]{2,1,0:T(8,128)(2,1)}), bf16[128,32,256]{2,1,0:T(8,128)(2,1)S(1)}, u32[]{:S(2)}, u32[]{:S(2)}) %all-to-all-start.1) | async-done | bytes 2097184 | tf_op jit(solution)/shard_map/all_to_all | solution.py:328
  109.4 0.0 copy-start.2
  109.4 6.4 %d_tri.1 = bf16[128,32,256]{2,1,0:T(8,128)(2,1)S(1)} custom-call(bf16[128,32,256]{2,1,0:T(8,128)(2,1)S(1)} %all-to-all-done.1.tri, bf16[32,128,256]{2,1,0:T(8,128)(2,1)} %get-tuple-element.23.d_proj, f32[1,128]{1,0:T(1,128)} %bitcast.27, bf16[128,128]{1,0:T(8,128)(2,1)} %w_out.3), custom_call_target="tpu_custom_call" | custom-call | flops 268435456 | bytes 8388608 | tf_op jit(solution)/shard_map/d_tri/pallas_call | solution.py:66
  115.9 0.0 copy-done.2
  115.9 0.0 copy-start.1
  115.9 34.3 %all_to_all.31 = bf16[128,32,256]{2,1,0:T(8,128)(2,1)S(1)} all-to-all(bf16[128,32,256]{2,1,0:T(8,128)(2,1)S(1)} %d_tri.1), channel_id=1, replica_groups=mesh['grp'=4,'row'=32] {'grp','row'}, dimensions={0} | all-to-all | bytes 4194304 | tf_op jit(solution)/shard_map/all_to_all | solution.py:328
  150.2 0.0 copy-done.1
  150.2 6.4 %d_edges.1 = bf16[4,32,2,32,256]{4,3,2,1,0:T(8,128)(2,1)} custom-call(bf16[4,32,2,32,256]{4,3,2,1,0:T(8,128)(2,1)S(1)} %bitcast.11, bf16[4,1024,256]{2,1,0:T(8,128)(2,1)S(1)} %bitcast.12), custom_call_target="tpu_custom_call" | custom-call | flops 4294967296 | bytes 10485760 | tf_op jit(solution)/shard_map/d_edges/pallas_call | solution.py:66
  156.6 6.0 %all-to-all-start.3 = ((bf16[128,2,32,256]{3,2,1,0:T(8,128)(2,1)}), bf16[128,2,32,256]{3,2,1,0:T(8,128)(2,1)}, u32[]{:S(2)}, u32[]{:S(2)}) async-start(bf16[128,2,32,256]{3,2,1,0:T(8,128)(2,1)} %bitcast.14), calls=%async_computation.3 | async-start | bytes 8388608 | tf_op jit(solution)/shard_map/all_to_all | solution.py:328
  162.6 8.1 %factors.1 = bf16[32,512,256]{2,1,0:T(8,128)(2,1)} custom-call(bf16[32,128,256]{2,1,0:T(8,128)(2,1)} %get-tuple-element.21.pair_t, s32[1024]{0:T(1024)} %row_tokens.3, s32[8,128]{1,0:T(8,128)} %bitcast.16, f32[1,128]{1,0:T(1,128)} %bitcast.19, f32[1,128]{1,0:T(1,128)} %bitcast.24, bf16[128,512]{1,0:T(8,128)(2,1)} %w_in.5), custom_call_target="tpu_custom_call" | custom-call | flops 1073741824 | bytes 10485760 | tf_op jit(solution)/shard_map/factors/pallas_call | solution.py:66
  170.7 13.8 %update.1 = (bf16[32,256,128]{2,1,0:T(8,128)(2,1)}, bf16[32,128,256]{2,1,0:T(8,128)(2,1)}, f32[128,128]{1,0:T(8,128)S(1)}, f32[128,128]{1,0:T(8,128)S(1)}, f32[128,128]{1,0:T(8,128)S(1)}) custom-call(bf16[128,32,256]{2,1,0:T(8,128)(2,1)} %copy-done.2, bf16[32,128,256]{2,1,0:T(8,128)(2,1)} %get-tuple-element.21.pair_t, bf16[32,256,128]{2,1,0:T(8,128)(2,1)} %d_update.3, ...), custom_call_target="tpu_custom_call" | custom-call | flops 1342177280 | bytes 16777216 | tf_op jit(solution)/shard_map/update/pallas_call | solution.py:66
  184.6 29.2 %all-to-all-done.3.d_edges = bf16[128,2,32,256]{3,2,1,0:T(8,128)(2,1)} async-done(((bf16[128,2,32,256]{3,2,1,0:T(8,128)(2,1)}), bf16[128,2,32,256]{3,2,1,0:T(8,128)(2,1)}, u32[]{:S(2)}, u32[]{:S(2)}) %all-to-all-start.3) | async-done | bytes 4194336 | tf_op jit(solution)/shard_map/all_to_all | solution.py:328
  213.8 11.1 %back.1 = (bf16[32,256,128]{2,1,0:T(8,128)(2,1)}, bf16[128,8,128]{2,1,0:T(8,128)(2,1)S(1)}) custom-call(bf16[128,2,32,256]{3,2,1,0:T(8,128)(2,1)} %all-to-all-done.3.d_edges, bf16[32,128,256]{2,1,0:T(8,128)(2,1)} %get-tuple-element.21.pair_t, bf16[32,128,256]{2,1,0:T(8,128)(2,1)} %get-tuple-element.24.d_gate, bf16[32,512,256]{2,1,0:T(8,128)(2,1)} %factors.1, ...), custom_call_target="tpu_custom_call" | custom-call | flops 3489660928 | bytes 16777216 | tf_op jit(solution)/shard_map/back/pallas_call | solution.py:66
  224.9 16.5 %all_to_all.32.arrived = bf16[128,8,128]{2,1,0:T(8,128)(2,1)S(1)} all-to-all(bf16[128,8,128]{2,1,0:T(8,128)(2,1)S(1)} %get-tuple-element.29), channel_id=1, replica_groups=mesh['grp'=4,'row'=32] {'grp','row'}, dimensions={0} | all-to-all | bytes 524288 | tf_op jit(solution)/shard_map/all_to_all | solution.py:328
  241.4 0.2 total.1
  241.6 14.9 %all_to_all.33.sums = bf16[128,8,128]{2,1,0:T(8,128)(2,1)S(1)} all-to-all(bf16[128,8,128]{2,1,0:T(8,128)(2,1)S(1)} %total.1), channel_id=1, replica_groups=mesh['grp'=4,'row'=32] {'grp','row'}, dimensions={0} | all-to-all | bytes 524288 | tf_op jit(solution)/shard_map/all_to_all | solution.py:328
  256.4 0.9 unpack.1
Async XLA Ops:
  70.1 4.5 %copy-start = (bf16[128,2,32,256]{3,2,1,0:T(8,128)(2,1)}, bf16[128,2,32,256]{3,2,1,0:T(8,128)(2,1)S(1)}, u32[]{:S(2)}) copy-start(bf16[128,2,32,256]{3,2,1,0:T(8,128)(2,1)S(1)} %all_to_all.30) | copy-start | bytes 12582916
  74.6 34.9 %all-to-all-start.1 = ((bf16[128,32,256]{2,1,0:T(8,128)(2,1)}), bf16[128,32,256]{2,1,0:T(8,128)(2,1)S(1)}, u32[]{:S(2)}, u32[]{:S(2)}) async-start(bf16[128,32,256]{2,1,0:T(8,128)(2,1)} %bitcast.13), calls=%async_computation.1 | async-start | bytes 4194304 | tf_op jit(solution)/shard_map/all_to_all | solution.py:328
  109.4 6.5 %copy-start.2 = (bf16[128,32,256]{2,1,0:T(8,128)(2,1)}, bf16[128,32,256]{2,1,0:T(8,128)(2,1)S(1)}, u32[]{:S(2)}) copy-start(bf16[128,32,256]{2,1,0:T(8,128)(2,1)S(1)} %all-to-all-done.1.tri) | copy-start | bytes 6291460
  115.9 34.3 %copy-start.1 = (bf16[128,2,32,256]{3,2,1,0:T(8,128)(2,1)S(1)}, bf16[128,2,32,256]{3,2,1,0:T(8,128)(2,1)}, u32[]{:S(2)}) copy-start(bf16[128,2,32,256]{3,2,1,0:T(8,128)(2,1)} %copy-done) | copy-start | bytes 12582916
  156.6 57.2 %all-to-all-start.3 = ((bf16[128,2,32,256]{3,2,1,0:T(8,128)(2,1)}), bf16[128,2,32,256]{3,2,1,0:T(8,128)(2,1)}, u32[]{:S(2)}, u32[]{:S(2)}) async-start(bf16[128,2,32,256]{3,2,1,0:T(8,128)(2,1)} %bitcast.14), calls=%async_computation.3 | async-start | bytes 8388608 | tf_op jit(solution)/shard_map/all_to_all | solution.py:328

commit v5 on v4

--- a/solution.py
+++ b/solution.py
@@ -116,7 +116,9 @@
         edges[:, side] = swap_rows(jnp.stack(sides[side]))
 
 
-def cotangent_kernel(pair, d_update, gain, bias, w_gate, d_proj, pair_t, wg_t, cols):
+def cotangent_kernel(
+    pair, d_update, gain, bias, w_gate, o_gain, w_out, grads, pair_t, wg_t, cols
+):
     width = pair_t.shape[2]
 
     @pl.when(pl.program_id(0) == 0)
@@ -124,6 +126,7 @@
         wg_t[...] = w_gate[...].T
         cols[0] = columns(gain[...], width)
         cols[1] = columns(bias[...], width)
+        cols[2] = columns(o_gain[...], width)
 
     for r in range(RB):
         x_t = pair[r].T
@@ -131,7 +134,9 @@
         hat, _ = norm0(x_t.astype(F32))
         normed = (hat * cols[0] + cols[1]).astype(BF16)
         gate = sigmoid(dot(wg_t[...], normed))
-        d_proj[r] = (d_update[r].T.astype(F32) * gate).astype(BF16)
+        d_proj = (d_update[r].T.astype(F32) * gate).astype(BF16)
+        grad = dot(w_out[...], d_proj) * cols[2]
+        grads[r] = grad - jnp.mean(grad, axis=0, keepdims=True)
 
 
 def triangle_kernel(left, right, out):
@@ -142,20 +147,15 @@
         out[h] = dot(left_t, right[h].reshape(depth, width)).astype(BF16)
 
 
-def d_tri_kernel(tri, d_proj, gain, w_out, d_tri, cols):
-    width = tri.shape[2]
-
-    @pl.when(pl.program_id(0) == 0)
-    def _():
-        cols[...] = columns(gain[...], width)
-
+def d_tri_kernel(tri, grads, d_tri):
     arrived = swap_rows(tri[...])
-    grads = []
+    rows = []
     for r in range(RB):
         hat, inv = norm0(arrived[r].astype(F32))
-        grad = dot(w_out[...], d_proj[r]) * cols[...]
-        grads.append(norm0_back(grad, hat, inv).astype(BF16))
-    d_tri[...] = swap_rows(jnp.stack(grads))
+        grad = grads[r]
+        along = jnp.mean(grad * hat, axis=0, keepdims=True)
+        rows.append((inv * (grad - hat * along)).astype(BF16))
+    d_tri[...] = swap_rows(jnp.stack(rows))
 
 
 def update_kernel(
@@ -371,13 +371,16 @@
         in_hbm=(0, 2, 3, 4, 5),
     )
     chan_edges = exchange(edges)
-    d_proj, pair_t = call(
+    grads, pair_t = call(
         cotangent_kernel, "cotangent", (steps,),
-        [rowblock, rowblock, vec, vec, square],
-        [(chanblock, pltpu.HBM(t_shape.shape, BF16))] * 2,
-        [pltpu.VMEM((chans, hidden), BF16), pltpu.VMEM((2, chans, tile_cols), F32)],
+        [rowblock, rowblock, vec, vec, square, vec, square],
+        [
+            (chanblock, pltpu.HBM(t_shape.shape, F32)),
+            (chanblock, pltpu.HBM(t_shape.shape, BF16)),
+        ],
+        [pltpu.VMEM((chans, hidden), BF16), pltpu.VMEM((3, chans, tile_cols), F32)],
         2 * positions * chans * hidden, 8 * positions * chans,
-        (pair, d_update, gain, bias, w_gate),
+        (pair, d_update, gain, bias, w_gate, o_gain, w_out),
     )
     chan_edges = chan_edges.reshape(groups, rows, 2, tile_rows, tile_cols)
     (triangle,) = call(
@@ -400,16 +403,14 @@
     tri = exchange(triangle.reshape(devices, tile_rows, tile_cols))
     (d_tri,) = call(
         d_tri_kernel, "d_tri", (steps,),
-        [triblock, chanblock, vec, square],
+        [triblock, chanblock],
         [
             (triblock, sds((hidden, tile_rows, tile_cols), BF16)),
         ],
-        [
-            pltpu.VMEM((hidden, tile_cols), F32),
-        ],
+        [],
         2 * positions * chans * hidden, 8 * positions * chans,
-        (tri, d_proj, o_gain, w_out),
-        in_hbm=(1, 2, 3),
+        (tri, grads),
+        in_hbm=(1,),
     )
     chan_d_tri = exchange(d_tri)
     update, d_gate, sum_gate, sum_out, sum_norm = call(

time: 258 us -> 257 us (level)
  no operation moved by 1% of the time
where the time goes in v5:
time: 257 us
  blocking collectives  128 us (50%)
  Pallas kernels  64.2 us (25%)
  waiting for transfers between devices  51.9 us (20%)
  starting transfers between devices  11.5 us (4%)
    all_to_all x4, blocking collectives, exchange(): return lax.all_to_all(chunks, AXES, split_axis=0, concat_axis=0, tiled=True)  128 us
    pallas_call x10, Pallas kernels, call(): pl.pallas_call(kernel, name=name, grid=grid, in_specs=ins, out_specs=[spe...  64.2 us
    all_to_all x2, waiting for transfers between devices, exchange(): return lax.all_to_all(chunks, AXES, split_axis=0, concat_axis=0, tiled=True)  51.9 us
    all_to_all x2, starting transfers between devices, exchange(): return lax.all_to_all(chunks, AXES, split_axis=0, concat_axis=0, tiled=True)  11.5 us
  transfers between devices with their start and end apart: 2, of which 2 were waited for; matrix products, arithmetic and copies ran while one was open for 0% of the time, Pallas kernels for 11%

profile of v5, /device:TPU:1, one launch (start us, length us, event | category | flops | bytes accessed | tf_op | source)
XLA Modules:
  0.0 256.6 jit_solution(10633949463290748313)
XLA Ops:
  0.6 6.7 %edges.1 = bf16[128,2,32,256]{3,2,1,0:T(8,128)(2,1)S(1)} custom-call(bf16[32,256,128]{2,1,0:T(8,128)(2,1)} %pair.3, s32[1024]{0:T(1024)} %row_tokens.3, s32[8,128]{1,0:T(8,128)} %bitcast.15, f32[1,128]{1,0:T(1,128)} %bitcast.17, f32[1,128]{1,0:T(1,128)} %bitcast.22, bf16[128,512]{1,0:T(8,128)(2,1)} %w_in.5), custom_call_target="tpu_custom_call" | custom-call | flops 1073741824 | bytes 16777216 | tf_op jit(solution)/shard_map/edges/pallas_call | solution.py:66
  7.3 62.7 %all_to_all.30 = bf16[128,2,32,256]{3,2,1,0:T(8,128)(2,1)S(1)} all-to-all(bf16[128,2,32,256]{3,2,1,0:T(8,128)(2,1)S(1)} %edges.1), channel_id=1, replica_groups=mesh['grp'=4,'row'=32] {'grp','row'}, dimensions={0} | all-to-all | bytes 8388608 | tf_op jit(solution)/shard_map/all_to_all | solution.py:328
  70.1 0.0 copy-start
  70.1 4.5 %triangle.1 = bf16[4,1024,256]{2,1,0:T(8,128)(2,1)} custom-call(bf16[4,32,2,32,256]{4,3,2,1,0:T(8,128)(2,1)S(1)} %bitcast.9, bf16[4,32,2,32,256]{4,3,2,1,0:T(8,128)(2,1)S(1)} %bitcast.10), custom_call_target="tpu_custom_call" | custom-call | flops 2147483648 | bytes 6291456 | tf_op jit(solution)/shard_map/triangle/pallas_call | solution.py:66
  74.6 0.0 copy-done
  74.6 5.5 %all-to-all-start.1 = ((bf16[128,32,256]{2,1,0:T(8,128)(2,1)}), bf16[128,32,256]{2,1,0:T(8,128)(2,1)S(1)}, u32[]{:S(2)}, u32[]{:S(2)}) async-start(bf16[128,32,256]{2,1,0:T(8,128)(2,1)} %bitcast.13), calls=%async_computation.1 | async-start | bytes 4194304 | tf_op jit(solution)/shard_map/all_to_all | solution.py:328
  80.1 6.7 %cotangent.1 = (f32[32,128,256]{2,1,0:T(8,128)}, bf16[32,128,256]{2,1,0:T(8,128)(2,1)}) custom-call(bf16[32,256,128]{2,1,0:T(8,128)(2,1)} %pair.3, bf16[32,256,128]{2,1,0:T(8,128)(2,1)} %d_update.3, f32[1,128]{1,0:T(1,128)} %bitcast.18, f32[1,128]{1,0:T(1,128)} %bitcast.23, bf16[128,128]{1,0:T(8,128)(2,1)} %w_gate.5, f32[1,128]{1,0:T(1,128)} %bitcast.27, ...), custom_call_target="tpu_custom_call" | custom-call | flops 268435456 | bytes 8388608 | tf_op jit(solution)/shard_map/cotangent/pallas_call | solution.py:66
  86.8 22.6 %all-to-all-done.1.tri = bf16[128,32,256]{2,1,0:T(8,128)(2,1)S(1)} async-done(((bf16[128,32,256]{2,1,0:T(8,128)(2,1)}), bf16[128,32,256]{2,1,0:T(8,128)(2,1)S(1)}, u32[]{:S(2)}, u32[]{:S(2)}) %all-to-all-start.1) | async-done | bytes 2097184 | tf_op jit(solution)/shard_map/all_to_all | solution.py:328
  109.4 0.0 copy-start.2
  109.4 5.8 %d_tri.1 = bf16[128,32,256]{2,1,0:T(8,128)(2,1)S(1)} custom-call(bf16[128,32,256]{2,1,0:T(8,128)(2,1)S(1)} %all-to-all-done.1.tri, f32[32,128,256]{2,1,0:T(8,128)} %get-tuple-element.23.grads), custom_call_target="tpu_custom_call" | custom-call | flops 268435456 | bytes 8388608 | tf_op jit(solution)/shard_map/d_tri/pallas_call | solution.py:66
  115.2 0.0 copy-done.2
  115.2 0.0 copy-start.1
  115.3 34.3 %all_to_all.31 = bf16[128,32,256]{2,1,0:T(8,128)(2,1)S(1)} all-to-all(bf16[128,32,256]{2,1,0:T(8,128)(2,1)S(1)} %d_tri.1), channel_id=1, replica_groups=mesh['grp'=4,'row'=32] {'grp','row'}, dimensions={0} | all-to-all | bytes 4194304 | tf_op jit(solution)/shard_map/all_to_all | solution.py:328
  149.5 0.0 copy-done.1
  149.5 6.4 %d_edges.1 = bf16[4,32,2,32,256]{4,3,2,1,0:T(8,128)(2,1)} custom-call(bf16[4,32,2,32,256]{4,3,2,1,0:T(8,128)(2,1)S(1)} %bitcast.11, bf16[4,1024,256]{2,1,0:T(8,128)(2,1)S(1)} %bitcast.12), custom_call_target="tpu_custom_call" | custom-call | flops 4294967296 | bytes 10485760 | tf_op jit(solution)/shard_map/d_edges/pallas_call | solution.py:66
  155.9 6.0 %all-to-all-start.3 = ((bf16[128,2,32,256]{3,2,1,0:T(8,128)(2,1)}), bf16[128,2,32,256]{3,2,1,0:T(8,128)(2,1)}, u32[]{:S(2)}, u32[]{:S(2)}) async-start(bf16[128,2,32,256]{3,2,1,0:T(8,128)(2,1)} %bitcast.14), calls=%async_computation.3 | async-start | bytes 8388608 | tf_op jit(solution)/shard_map/all_to_all | solution.py:328
  161.9 8.1 %factors.1 = bf16[32,512,256]{2,1,0:T(8,128)(2,1)} custom-call(bf16[32,128,256]{2,1,0:T(8,128)(2,1)} %get-tuple-element.21.pair_t, s32[1024]{0:T(1024)} %row_tokens.3, s32[8,128]{1,0:T(8,128)} %bitcast.16, f32[1,128]{1,0:T(1,128)} %bitcast.19, f32[1,128]{1,0:T(1,128)} %bitcast.24, bf16[128,512]{1,0:T(8,128)(2,1)} %w_in.5), custom_call_target="tpu_custom_call" | custom-call | flops 1073741824 | bytes 10485760 | tf_op jit(solution)/shard_map/factors/pallas_call | solution.py:66
  170.1 13.8 %update.1 = (bf16[32,256,128]{2,1,0:T(8,128)(2,1)}, bf16[32,128,256]{2,1,0:T(8,128)(2,1)}, f32[128,128]{1,0:T(8,128)S(1)}, f32[128,128]{1,0:T(8,128)S(1)}, f32[128,128]{1,0:T(8,128)S(1)}) custom-call(bf16[128,32,256]{2,1,0:T(8,128)(2,1)} %copy-done.2, bf16[32,128,256]{2,1,0:T(8,128)(2,1)} %get-tuple-element.21.pair_t, bf16[32,256,128]{2,1,0:T(8,128)(2,1)} %d_update.3, ...), custom_call_target="tpu_custom_call" | custom-call | flops 1342177280 | bytes 16777216 | tf_op jit(solution)/shard_map/update/pallas_call | solution.py:66
  183.9 29.2 %all-to-all-done.3.d_edges = bf16[128,2,32,256]{3,2,1,0:T(8,128)(2,1)} async-done(((bf16[128,2,32,256]{3,2,1,0:T(8,128)(2,1)}), bf16[128,2,32,256]{3,2,1,0:T(8,128)(2,1)}, u32[]{:S(2)}, u32[]{:S(2)}) %all-to-all-start.3) | async-done | bytes 4194336 | tf_op jit(solution)/shard_map/all_to_all | solution.py:328
  213.2 11.1 %back.1 = (bf16[32,256,128]{2,1,0:T(8,128)(2,1)}, bf16[128,8,128]{2,1,0:T(8,128)(2,1)S(1)}) custom-call(bf16[128,2,32,256]{3,2,1,0:T(8,128)(2,1)} %all-to-all-done.3.d_edges, bf16[32,128,256]{2,1,0:T(8,128)(2,1)} %get-tuple-element.21.pair_t, bf16[32,128,256]{2,1,0:T(8,128)(2,1)} %get-tuple-element.24.d_gate, bf16[32,512,256]{2,1,0:T(8,128)(2,1)} %factors.1, ...), custom_call_target="tpu_custom_call" | custom-call | flops 3489660928 | bytes 16777216 | tf_op jit(solution)/shard_map/back/pallas_call | solution.py:66
  224.2 16.5 %all_to_all.32.arrived = bf16[128,8,128]{2,1,0:T(8,128)(2,1)S(1)} all-to-all(bf16[128,8,128]{2,1,0:T(8,128)(2,1)S(1)} %get-tuple-element.29), channel_id=1, replica_groups=mesh['grp'=4,'row'=32] {'grp','row'}, dimensions={0} | all-to-all | bytes 524288 | tf_op jit(solution)/shard_map/all_to_all | solution.py:328
  240.8 0.2 total.1
  240.9 14.9 %all_to_all.33.sums = bf16[128,8,128]{2,1,0:T(8,128)(2,1)S(1)} all-to-all(bf16[128,8,128]{2,1,0:T(8,128)(2,1)S(1)} %total.1), channel_id=1, replica_groups=mesh['grp'=4,'row'=32] {'grp','row'}, dimensions={0} | all-to-all | bytes 524288 | tf_op jit(solution)/shard_map/all_to_all | solution.py:328
  255.8 0.9 unpack.1
Async XLA Ops:
  70.1 4.5 %copy-start = (bf16[128,2,32,256]{3,2,1,0:T(8,128)(2,1)}, bf16[128,2,32,256]{3,2,1,0:T(8,128)(2,1)S(1)}, u32[]{:S(2)}) copy-start(bf16[128,2,32,256]{3,2,1,0:T(8,128)(2,1)S(1)} %all_to_all.30) | copy-start | bytes 12582916
  74.6 34.9 %all-to-all-start.1 = ((bf16[128,32,256]{2,1,0:T(8,128)(2,1)}), bf16[128,32,256]{2,1,0:T(8,128)(2,1)S(1)}, u32[]{:S(2)}, u32[]{:S(2)}) async-start(bf16[128,32,256]{2,1,0:T(8,128)(2,1)} %bitcast.13), calls=%async_computation.1 | async-start | bytes 4194304 | tf_op jit(solution)/shard_map/all_to_all | solution.py:328
  109.4 5.8 %copy-start.2 = (bf16[128,32,256]{2,1,0:T(8,128)(2,1)}, bf16[128,32,256]{2,1,0:T(8,128)(2,1)S(1)}, u32[]{:S(2)}) copy-start(bf16[128,32,256]{2,1,0:T(8,128)(2,1)S(1)} %all-to-all-done.1.tri) | copy-start | bytes 6291460
  115.2 34.3 %copy-start.1 = (bf16[128,2,32,256]{3,2,1,0:T(8,128)(2,1)S(1)}, bf16[128,2,32,256]{3,2,1,0:T(8,128)(2,1)}, u32[]{:S(2)}) copy-start(bf16[128,2,32,256]{3,2,1,0:T(8,128)(2,1)} %copy-done) | copy-start | bytes 12582916
  155.9 57.2 %all-to-all-start.3 = ((bf16[128,2,32,256]{3,2,1,0:T(8,128)(2,1)}), bf16[128,2,32,256]{3,2,1,0:T(8,128)(2,1)}, u32[]{:S(2)}, u32[]{:S(2)}) async-start(bf16[128,2,32,256]{3,2,1,0:T(8,128)(2,1)} %bitcast.14), calls=%async_computation.3 | async-start | bytes 8388608 | tf_op jit(solution)/shard_map/all_to_all | solution.py:328
